TPU v7x, 512 devices: a whole 4x8x8 slice. The times are simulated.
512 devices in a mesh: il: 64 (over z_hi, y, core), xl: 8 (over z_lo, x).
Axes of the slice: x: 4, y: 8, z: 8 (z_hi: 4, z_lo: 2; z = z_hi * 2 + z_lo), core: 2. Of those that a mesh axis runs over, the one named last changes fastest.
Arguments:
- solution: float32 [256, 512, 512], P('il', 'xl'), may hold values from -6 to 6
- residual: float32 [256, 512, 512], P('il', 'xl'), may hold values from -30 to 30
- direction: float32 [256, 512, 512], P('il', 'xl'), may hold values from -30 to 30
- slope_il: float32 [256, 512, 512], P('il', 'xl'), may hold values from -1.5 to 1.5
- slope_xl: float32 [256, 512, 512], P('il', 'xl'), may hold values from -1.5 to 1.5
- weights: float32 [256, 512, 512], P('il', 'xl'), may hold values from 0.2 to 1
Outputs:
- new_solution: float32 [256, 512, 512], P('il', 'xl')
- new_residual: float32 [256, 512, 512], P('il', 'xl')
- new_direction: float32 [256, 512, 512], P('il', 'xl')
All inputs are finite; a program needn't handle non-finite values.
Results may differ from a plain program's by a relative error of at most 0.00002.
Values sent between devices are 32-bit elements; how exact they have to be, the bound alone decides.
A program may use at most 64 MiB of HBM per device.

v0:
```python
import jax
import jax.numpy as jnp
from jax import lax
from jax.sharding import Mesh
from jax.sharding import PartitionSpec as P

IL = ("il_0", "il_1", "il_2")
XL = ("xl_0", "xl_1")
IL_XL = ("il_0", "il_1", "il_2", "xl_0", "xl_1")


damping = 0.3


def shifted(value, axis, by):
    length = lax.axis_size(axis)
    pairs = [(i, i + by) for i in range(length) if 0 <= i + by < length]
    return lax.ppermute(value, axis, pairs)


def over_axes(value, axes):
    for axis in axes:
        value = lax.psum(value, axis)
    return value


def time_diff(field):
    padded = jnp.pad(field, ((0, 0), (0, 0), (1, 1)))
    return 0.5 * (padded[:, :, 2:] - padded[:, :, :-2])


def normal_apply(direction, slope_il, slope_xl, weights):
    il_rows = direction.shape[0]
    xl_rows = direction.shape[1]
    total_il = il_rows * lax.axis_size(IL)
    total_xl = xl_rows * lax.axis_size(XL)
    start_il = lax.axis_index(IL) * il_rows
    start_xl = lax.axis_index(XL) * xl_rows
    squared = weights * weights
    next_il = shifted(direction[:1], IL, -1)
    next_xl = shifted(direction[:, :1], XL, -1)
    ahead_il = jnp.concatenate([direction[1:], next_il], 0)
    ahead_xl = jnp.concatenate([direction[:, 1:], next_xl], 1)
    slope_t = time_diff(direction)
    keep_il = (start_il + jnp.arange(il_rows) < total_il - 1)[:, None, None]
    keep_xl = (start_xl + jnp.arange(xl_rows) < total_xl - 1)[None, :, None]
    flux_il = jnp.where(keep_il, squared * (ahead_il - direction - slope_il * slope_t), 0.0)
    flux_xl = jnp.where(keep_xl, squared * (ahead_xl - direction - slope_xl * slope_t), 0.0)
    prev_il = shifted(flux_il[-1:], IL, 1)
    prev_xl = shifted(flux_xl[:, -1:], XL, 1)
    behind_il = jnp.concatenate([prev_il, flux_il[:-1]], 0)
    behind_xl = jnp.concatenate([prev_xl, flux_xl[:, :-1]], 1)
    term_il = behind_il - flux_il + time_diff(slope_il * flux_il)
    term_xl = behind_xl - flux_xl + time_diff(slope_xl * flux_xl)
    return term_il + term_xl + damping * direction


def body(solution, residual, direction, slope_il, slope_xl, weights):
    image = normal_apply(direction, slope_il, slope_xl, weights)
    norm_old, along, cross_term, image_norm = (
        over_axes(jnp.sum(residual * residual), IL_XL),
        over_axes(jnp.sum(direction * image), IL_XL),
        over_axes(jnp.sum(residual * image), IL_XL),
        over_axes(jnp.sum(image * image), IL_XL),
    )
    alpha = norm_old / along
    new_residual = residual - alpha * image
    norm_new = norm_old - 2.0 * alpha * cross_term + alpha * alpha * image_norm
    new_solution = solution + alpha * direction
    new_direction = new_residual + norm_new / norm_old * direction
    return (new_solution, new_residual, new_direction)


def solution(mesh):
    torus = Mesh(mesh.devices.reshape(4, 8, 2, 2, 4), ("il_0", "il_1", "il_2", "xl_0", "xl_1"))
    return jax.shard_map(
        body,
        mesh=torus,
        in_specs=(
            P(IL, XL, None),
            P(IL, XL, None),
            P(IL, XL, None),
            P(IL, XL, None),
            P(IL, XL, None),
            P(IL, XL, None),
        ),
        out_specs=(P(IL, XL, None), P(IL, XL, None), P(IL, XL, None)),
        check_vma=False,
    )
```

profile of v0, /device:TPU:8, one launch (start us, length us, event | category | flops | bytes accessed | tf_op | source)
XLA Modules:
  0.0 85.6 jit_solution(10179543610063257132)
XLA Ops:
  0.6 0.8 slice.51
  1.5 0.0 copy-start
  1.5 1.4 %collective-permute-start.2 = (f32[4,1,512]{2,1,0:T(1,128)S(1)}, f32[4,1,512]{2,1,0:T(1,128)S(1)}, u32[]{:S(2)}, u32[]{:S(2)}) collective-permute-start(f32[4,1,512]{2,1,0:T(1,128)S(1)} %slice.51), channel_id=1, source_target_pairs={{1,0},{2,1},{3,2},{4,3},{5,4},{6,5},{7,6},{9,8},{10,9},{11,10},{12... | collective-permute-start | bytes 24584 | tf_op jit(solution)/shard_map/ppermute | solution.py:18
  2.9 0.9 %slice.43 = f32[1,64,512]{2,1,0:T(8,128)S(1)} slice(f32[4,64,512]{2,1,0:T(8,128)} %param.8), slice={[0:1], [0:64], [0:512]} | slice | bytes 262144 | tf_op jit(solution)/shard_map/slice | solution.py:40
  3.8 1.9 %collective-permute-start = (f32[1,64,512]{2,1,0:T(8,128)S(1)}, f32[1,64,512]{2,1,0:T(8,128)S(1)}, u32[]{:S(2)}, u32[]{:S(2)}) collective-permute-start(f32[1,64,512]{2,1,0:T(8,128)S(1)} %slice.43), channel_id=1, source_target_pairs={{8,0},{16,8},{24,16},{32,24},{40,32},{48,40},{56,48},{64,56},{72,6... | collective-permute-start | bytes 393224 | tf_op jit(solution)/shard_map/ppermute | solution.py:18
  5.8 0.0 copy-start.3
  5.8 0.0 copy-done
  5.8 0.0 slice-start
  5.8 0.0 copy-start.2
  5.8 0.1 slice.50
  5.9 1.2 %collective-permute-done.2 = f32[4,1,512]{2,1,0:T(1,128)S(1)} collective-permute-done((f32[4,1,512]{2,1,0:T(1,128)S(1)}, f32[4,1,512]{2,1,0:T(1,128)S(1)}, u32[]{:S(2)}, u32[]{:S(2)}) %collective-permute-start.2) | collective-permute-done | bytes 8224 | tf_op jit(solution)/shard_map/ppermute | solution.py:18
  7.1 1.1 %collective-permute-done = f32[1,64,512]{2,1,0:T(8,128)S(1)} collective-permute-done((f32[1,64,512]{2,1,0:T(8,128)S(1)}, f32[1,64,512]{2,1,0:T(8,128)S(1)}, u32[]{:S(2)}, u32[]{:S(2)}) %collective-permute-start) | collective-permute-done | bytes 131104 | tf_op jit(solution)/shard_map/ppermute | solution.py:18
  8.2 0.0 copy-done.3
  8.2 0.0 slice-done
  8.3 0.0 copy-done.2
  8.3 1.7 %fusion.19 = (f32[4,64,512]{2,1,0:T(8,128)S(1)}, f32[4,64,512]{2,1,0:T(8,128)S(1)}, f32[4,64,512]{2,1,0:T(8,128)S(1)}, f32[4,64,512]{2,1,0:T(8,128)S(1)}) fusion(f32[4,64,512]{2,1,0:T(8,128)S(1)} %copy-done.2, f32[4,64,512]{2,1,0:T(8,128)S(1)} %copy-done, f32[1,64,512]{2,1,0:T(8,128)S(1)} %collective-permute-done, f32[3,64,512]{2,1,0:T(8,128)S(1)} %slice-done, ...), kind=kLoop, calls=%fused_computation.36 | loop fusion | flops 2490368 | bytes 5242948 | tf_op jit(solution)/shard_map/mul | solution.py:53
  10.0 0.0 copy-start.1
  10.0 3.9 %collective-permute-start.1 = (f32[1,64,512]{2,1,0:T(8,128)S(1)}, f32[1,64,512]{2,1,0:T(8,128)S(1)}, u32[]{:S(2)}, u32[]{:S(2)}) collective-permute-start(f32[1,64,512]{2,1,0:T(8,128)S(1)} %slice.56), channel_id=1, source_target_pairs={{0,8},{8,16},{16,24},{24,32},{32,40},{40,48},{48,56},{56,64},{64,7... | collective-permute-start | bytes 393224 | tf_op jit(solution)/shard_map/ppermute | solution.py:18
  13.9 4.5 %collective-permute-start.3 = (f32[4,1,512]{2,1,0:T(1,128)S(1)}, f32[4,1,512]{2,1,0:T(1,128)S(1)}, u32[]{:S(2)}, u32[]{:S(2)}) collective-permute-start(f32[4,1,512]{2,1,0:T(1,128)S(1)} %slice.58), channel_id=1, source_target_pairs={{0,1},{1,2},{2,3},{3,4},{4,5},{5,6},{6,7},{8,9},{9,10},{10,11},{11... | collective-permute-start | bytes 24584 | tf_op jit(solution)/shard_map/ppermute | solution.py:18
  18.5 1.3 %collective-permute-done.3 = f32[4,1,512]{2,1,0:T(1,128)S(1)} collective-permute-done((f32[4,1,512]{2,1,0:T(1,128)S(1)}, f32[4,1,512]{2,1,0:T(1,128)S(1)}, u32[]{:S(2)}, u32[]{:S(2)}) %collective-permute-start.3) | collective-permute-done | bytes 8224 | tf_op jit(solution)/shard_map/ppermute | solution.py:18
  19.8 0.0 collective-permute-done.1
  19.8 0.0 copy-done.1
  19.8 0.0 copy-start.4
  19.8 1.3 %multiply_reduce_fusion = (f32[]{:T(128)}, f32[]{:T(128)}, f32[]{:T(128)}, f32[]{:T(128)}, f32[4,64,512]{2,1,0:T(8,128)S(1)}) fusion(f32[4,64,512]{2,1,0:T(8,128)S(1)} %copy-done.1, f32[4,64,512]{2,1,0:T(8,128)S(1)} %copy-done, f32[4,64,512]{2,1,0:T(8,128)S(1)} %get-tuple-element.34, f32[4,64,512]{2,1,0:T(8,128)S(1)} %get-tuple-element.35, ...), kind=kLoop, calls=%fused_computation.27 | loop fusion | flops 2752508 | bytes 4718608 | tf_op jit(solution)/shard_map/reduce_sum | solution.py:64
  21.1 18.3 %all-reduce.5 = (f32[]{:T(128)}, f32[]{:T(128)}, f32[]{:T(128)}, f32[]{:T(128)}) all-reduce(f32[]{:T(128)} %get-tuple-element.5, f32[]{:T(128)} %get-tuple-element.6, f32[]{:T(128)} %get-tuple-element.4, f32[]{:T(128)} %get-tuple-element.3), channel_id=1, replica_groups=mesh['il_0'=4,'il_1'=8,'il_2'=2,'xl_0'=2,'xl_1'=4] {'il_0'}, use_global_device_ids=true, to_apply=%region_1.2 | all-reduce | flops 4 | bytes 32 | tf_op jit(solution)/shard_map/psum | solution.py:23
  39.4 18.9 %all-reduce.3 = (f32[]{:T(128)}, f32[]{:T(128)}, f32[]{:T(128)}, f32[]{:T(128)}) all-reduce(f32[]{:T(128)} %get-tuple-element.15, f32[]{:T(128)} %get-tuple-element.16, f32[]{:T(128)} %get-tuple-element.17, f32[]{:T(128)} %get-tuple-element.18), channel_id=1, replica_groups=mesh['il_0'=4,'il_1'=8,'il_2'=2,'xl_0'=2,'xl_1'=4] {'il_1'}, use_global_device_ids=true, to_apply=%region_2.3 | all-reduce | flops 4 | bytes 32 | tf_op jit(solution)/shard_map/psum | solution.py:23
  58.3 3.2 %all-reduce.7 = (f32[]{:T(128)}, f32[]{:T(128)}, f32[]{:T(128)}, f32[]{:T(128)}) all-reduce(f32[]{:T(128)} %get-tuple-element.7, f32[]{:T(128)} %get-tuple-element.8, f32[]{:T(128)} %get-tuple-element.9, f32[]{:T(128)} %get-tuple-element.10), channel_id=1, replica_groups=mesh['il_0'=4,'il_1'=8,'il_2'=2,'xl_0'=2,'xl_1'=4] {'il_2'}, use_global_device_ids=true, to_apply=%region_3.4 | all-reduce | flops 4 | bytes 32 | tf_op jit(solution)/shard_map/psum | solution.py:23
  61.5 7.6 %all-reduce.6 = (f32[]{:T(128)}, f32[]{:T(128)}, f32[]{:T(128)}, f32[]{:T(128)}) all-reduce(f32[]{:T(128)} %get-tuple-element.23, f32[]{:T(128)} %get-tuple-element.24, f32[]{:T(128)} %get-tuple-element.25, f32[]{:T(128)} %get-tuple-element.26), channel_id=1, replica_groups=mesh['il_0'=4,'il_1'=8,'il_2'=2,'xl_0'=2,'xl_1'=4] {'xl_0'}, use_global_device_ids=true, to_apply=%region_4.5 | all-reduce | flops 4 | bytes 32 | tf_op jit(solution)/shard_map/psum | solution.py:23
  69.1 11.2 %all-reduce.4 = (f32[]{:T(128)}, f32[]{:T(128)}, f32[]{:T(128)}, f32[]{:T(128)}) all-reduce(f32[]{:T(128)} %get-tuple-element.19, f32[]{:T(128)} %get-tuple-element.20, f32[]{:T(128)} %get-tuple-element.21, f32[]{:T(128)} %get-tuple-element.22), channel_id=1, replica_groups=mesh['il_0'=4,'il_1'=8,'il_2'=2,'xl_0'=2,'xl_1'=4] {'xl_1'}, use_global_device_ids=true, to_apply=%region_5.6 | all-reduce | flops 4 | bytes 32 | tf_op jit(solution)/shard_map/psum | solution.py:23
  84.3 0.0 copy-done.4
  84.3 1.4 %multiply_add_fusion = (f32[4,64,512]{2,1,0:T(8,128)}, f32[4,64,512]{2,1,0:T(8,128)}, f32[4,64,512]{2,1,0:T(8,128)}) fusion(f32[4,64,512]{2,1,0:T(8,128)S(1)} %copy-done, f32[]{:T(128)S(6)} %div.7, f32[4,64,512]{2,1,0:T(8,128)S(1)} %copy-done.1, f32[4,64,512]{2,1,0:T(8,128)S(1)} %get-tuple-element.29, f32[]{:T(128)S(6)} %div.6, f32[4,64,512]{2,1,0:T(8,128)S(1)} %copy-done.4), kind=kLoop, calls=%fused_computation.26 | loop fusion | flops 786432 | bytes 3670024 | tf_op jit(solution)/shard_map/add | solution.py:70
  (5 shorter events, 0.1 us)
Async XLA Ops:
  1.5 4.3 %copy-start = (f32[4,64,512]{2,1,0:T(8,128)S(1)}, f32[4,64,512]{2,1,0:T(8,128)}, u32[]{:S(2)}) copy-start(f32[4,64,512]{2,1,0:T(8,128)} %param.8) | copy-start | bytes 1572868
  1.5 5.7 %collective-permute-start.2 = (f32[4,1,512]{2,1,0:T(1,128)S(1)}, f32[4,1,512]{2,1,0:T(1,128)S(1)}, u32[]{:S(2)}, u32[]{:S(2)}) collective-permute-start(f32[4,1,512]{2,1,0:T(1,128)S(1)} %slice.51), channel_id=1, source_target_pairs={{1,0},{2,1},{3,2},{4,3},{5,4},{6,5},{7,6},{9,8},{10,9},{11,10},{12... | collective-permute-start | bytes 24584 | tf_op jit(solution)/shard_map/ppermute | solution.py:18
  3.8 4.4 %collective-permute-start = (f32[1,64,512]{2,1,0:T(8,128)S(1)}, f32[1,64,512]{2,1,0:T(8,128)S(1)}, u32[]{:S(2)}, u32[]{:S(2)}) collective-permute-start(f32[1,64,512]{2,1,0:T(8,128)S(1)} %slice.43), channel_id=1, source_target_pairs={{8,0},{16,8},{24,16},{32,24},{40,32},{48,40},{56,48},{64,56},{72,6... | collective-permute-start | bytes 393224 | tf_op jit(solution)/shard_map/ppermute | solution.py:18
  5.8 2.5 %copy-start.3 = (f32[4,64,512]{2,1,0:T(8,128)S(1)}, f32[4,64,512]{2,1,0:T(8,128)}, u32[]{:S(2)}) copy-start(f32[4,64,512]{2,1,0:T(8,128)} %param.11) | copy-start | bytes 1572868
  5.8 2.4 %slice-start = ((f32[4,64,512]{2,1,0:T(8,128)}), f32[3,64,512]{2,1,0:T(8,128)S(1)}, s32[]{:S(2)}) async-start(f32[4,64,512]{2,1,0:T(8,128)} %param.8), calls=%async_computation | async-start | bytes 786432 | tf_op jit(solution)/shard_map/slice | solution.py:42
  5.8 2.4 %copy-start.2 = (f32[4,64,512]{2,1,0:T(8,128)S(1)}, f32[4,64,512]{2,1,0:T(8,128)}, u32[]{:S(2)}) copy-start(f32[4,64,512]{2,1,0:T(8,128)} %param.9) | copy-start | bytes 1572868
  10.0 9.8 %copy-start.1 = (f32[4,64,512]{2,1,0:T(8,128)S(1)}, f32[4,64,512]{2,1,0:T(8,128)}, u32[]{:S(2)}) copy-start(f32[4,64,512]{2,1,0:T(8,128)} %param.7) | copy-start | bytes 1572868
  10.0 9.8 %collective-permute-start.1 = (f32[1,64,512]{2,1,0:T(8,128)S(1)}, f32[1,64,512]{2,1,0:T(8,128)S(1)}, u32[]{:S(2)}, u32[]{:S(2)}) collective-permute-start(f32[1,64,512]{2,1,0:T(8,128)S(1)} %slice.56), channel_id=1, source_target_pairs={{0,8},{8,16},{16,24},{24,32},{32,40},{40,48},{48,56},{56,64},{64,7... | collective-permute-start | bytes 393224 | tf_op jit(solution)/shard_map/ppermute | solution.py:18
  13.9 5.9 %collective-permute-start.3 = (f32[4,1,512]{2,1,0:T(1,128)S(1)}, f32[4,1,512]{2,1,0:T(1,128)S(1)}, u32[]{:S(2)}, u32[]{:S(2)}) collective-permute-start(f32[4,1,512]{2,1,0:T(1,128)S(1)} %slice.58), channel_id=1, source_target_pairs={{0,1},{1,2},{2,3},{3,4},{4,5},{5,6},{6,7},{8,9},{9,10},{10,11},{11... | collective-permute-start | bytes 24584 | tf_op jit(solution)/shard_map/ppermute | solution.py:18
  19.8 64.5 %copy-start.4 = (f32[4,64,512]{2,1,0:T(8,128)S(1)}, f32[4,64,512]{2,1,0:T(8,128)}, u32[]{:S(2)}) copy-start(f32[4,64,512]{2,1,0:T(8,128)} %param.6) | copy-start | bytes 1572868
where the time goes:
time: 86.1 us; the launch traced here: 85.6 us
  blocking collectives  59.2 us (69%)
  starting transfers between devices  11.7 us (14%)
  between operations  4.8 us (6%)
  other arithmetic  4.35 us (5%)
  waiting for transfers between devices  3.66 us (4%)
  local copies, waits for them, and re-layouts  1.9 us (2%)
    psum x5, blocking collectives, over_axes(): value = lax.psum(value, axis)  59.2 us
    ppermute x4, starting transfers between devices, shifted(): return lax.ppermute(value, axis, pairs)  11.7 us
    ppermute x4, waiting for transfers between devices, shifted(): return lax.ppermute(value, axis, pairs)  3.66 us
  transfers between devices with their start and end apart: 4, of which 3 were waited for; matrix products, arithmetic and copies ran while one was open for 1% of the time, Pallas kernels for 0%

commit v1 on v0

v1 whole, which is shorter than its diff:
```python
import jax
import jax.numpy as jnp
from jax import lax
from jax.experimental import pallas as pl
from jax.experimental.pallas import tpu as pltpu
from jax.sharding import PartitionSpec as P

damping = 0.3
F32 = jnp.float32
MESH_ID = pl.DeviceIdType.MESH

NIL, NXL = 64, 8
ROWS, COLS, NT = 4, 64, 512
STRIPS = COLS // 8
CHUNKS = 4
CHUNK = COLS // CHUNKS


def kernel(
    res_hbm, u_hbm, sil_hbm, sxl_hbm, w_hbm,
    image, coef,
    res, u, sil, sxl, w, fil, fx, h, xl_u_out, xl_u_in, xl_f_out, xl_f_in,
    msg, box,
    load_sem, us_send, us_recv, fs_send, fs_recv, x_send, x_recv, r_send, r_recv,
):
    il, xl = lax.axis_index("il"), lax.axis_index("xl")
    z_hi, y, core = il // 16, (il // 2) % 8, il % 2
    z_lo, x = xl // 4, xl % 4
    next_il = ((il + 1) % NIL, xl)
    prev_il = ((il + NIL - 1) % NIL, xl)
    next_xl = (il, (xl + 1) % NXL)
    prev_xl = (il, (xl + NXL - 1) % NXL)
    near = x * 2 + core
    z = z_hi * 2 + z_lo

    def peer(phase, d):
        if phase == 0:
            k = (near + d) % 8
            return (il - core + k % 2, z_lo * 4 + k // 2)
        if phase == 1:
            return (z_hi * 16 + ((y + d) % 8) * 2 + core, xl)
        k = (z + d) % 8
        return ((k // 2) * 16 + y * 2 + core, (k % 2) * 4 + x)

    order = (4, 3, 5, 2, 6, 1, 7)
    barrier = pltpu.get_barrier_semaphore()
    peers = [next_il, prev_il, next_xl, prev_xl]
    peers += [peer(phase, d) for phase in (2, 1, 0) for d in order]
    for other in peers:
        pl.semaphore_signal(barrier, inc=1, device_id=other, device_id_type=MESH_ID)

    loads = [
        pltpu.make_async_copy(u_hbm, u.at[pl.ds(0, ROWS), pl.ds(0, COLS)], load_sem.at[0]),
        pltpu.make_async_copy(w_hbm, w, load_sem.at[1]),
        pltpu.make_async_copy(sxl_hbm, sxl, load_sem.at[2]),
        pltpu.make_async_copy(sil_hbm, sil, load_sem.at[3]),
        pltpu.make_async_copy(res_hbm, res, load_sem.at[4]),
    ]
    for load in loads:
        load.start()
    pl.semaphore_wait(barrier, len(peers))

    u_copies = []
    for c in range(CHUNKS):
        u_copies.append(pltpu.make_async_remote_copy(
            u_hbm.at[0, pl.ds(c * CHUNK, CHUNK)],
            u.at[ROWS, pl.ds(c * CHUNK, CHUNK)],
            us_send.at[c], us_recv.at[c], prev_il, MESH_ID,
        ))
        u_copies[c].start()

    lane = lax.broadcasted_iota(jnp.int32, (8, NT), 1)
    sub = lax.broadcasted_iota(jnp.int32, (8, NT), 0)
    first_t, last_t = lane == 0, lane == NT - 1
    first_r, last_r = sub == 0, sub == 7

    def diff_t(v):
        ahead = jnp.where(last_t, 0.0, pltpu.roll(v, NT - 1, 1))
        behind = jnp.where(first_t, 0.0, pltpu.roll(v, 1, 1))
        return 0.5 * (ahead - behind)

    loads[0].wait()
    for i in range(ROWS):
        xl_u_out[i:i + 1] = u[i, 0:1]
    x_u = pltpu.make_async_remote_copy(
        xl_u_out, xl_u_in, x_send.at[0], x_recv.at[0], prev_xl, MESH_ID)
    x_u.start()
    loads[1].wait()
    loads[2].wait()
    for i in range(ROWS):
        tail = slice(COLS - 8, COLS)
        g = u[i, tail] + sxl[i, tail] * diff_t(u[i, tail])
        wt = w[i, tail]
        xl_f_out[i:i + 1] = g[7:8]
        xl_f_out[ROWS + i:ROWS + i + 1] = (wt * wt)[7:8]
    x_f = pltpu.make_async_remote_copy(
        xl_f_out, xl_f_in, x_send.at[1], x_recv.at[1], next_xl, MESH_ID)
    x_f.start()
    loads[3].wait()

    keep_il = jnp.where(il == NIL - 1, 0.0, 1.0).astype(F32)
    keep_xl = jnp.where(xl == NXL - 1, 0.0, 1.0).astype(F32)
    had_il = jnp.where(il == 0, 0.0, 1.0).astype(F32)
    had_xl = jnp.where(xl == 0, 0.0, 1.0).astype(F32)

    def crossline_flux(i, rows, next_row, last=False):
        here = u[i, rows]
        t = diff_t(here)
        wt = w[i, rows]
        sq = wt * wt
        ahead = jnp.where(last_r, next_row, pltpu.roll(here, 7, 0))
        slope = sxl[i, rows]
        flux = sq * (ahead - here - slope * t)
        if last:
            flux = jnp.where(last_r, keep_xl * flux, flux)
        return here, t, sq, flux, slope * flux

    def put_strip(i, jb, next_row, last=False):
        start = jb * 8 if last else pl.multiple_of(jb * 8, 8)
        rows = pl.ds(start, 8)
        here, t, sq, flux, part = crossline_flux(i, rows, next_row, last)
        fx[i, pl.ds(start + 8, 8)] = flux
        slope = sil[i, rows]
        if i < ROWS - 1:
            f = sq * (u[i + 1, rows] - here - slope * t)
            fil[i + 1, rows] = f
            h[i, rows] = part + slope * f
        else:
            fil[i + 1, rows] = here + slope * t
            h[i, rows] = part

    for i in range(ROWS):
        def strip(jb, _, i=i):
            put_strip(i, jb, u[i, pl.ds(jb * 8 + 8, 1)])
            return 0
        lax.fori_loop(0, STRIPS - 1, strip, 0, unroll=True)

    x_u.wait_recv()
    x_f.wait_recv()
    for i in range(ROWS):
        put_strip(i, STRIPS - 1, xl_u_in[i:i + 1], True)
        fx[i, 7:8] = had_xl * (xl_f_in[ROWS + i:ROWS + i + 1] * (u[i, 0:1] - xl_f_in[i:i + 1]))

    f_copies = []
    for c in range(CHUNKS):
        u_copies[c].wait_recv()
        for s in range(CHUNK // 8):
            rows = pl.ds(c * CHUNK + s * 8, 8)
            wt = w[ROWS - 1, rows]
            f = keep_il * (wt * wt * (u[ROWS, rows] - fil[ROWS, rows]))
            fil[ROWS, rows] = f
            h[ROWS - 1, rows] = h[ROWS - 1, rows] + sil[ROWS - 1, rows] * f
        f_copies.append(pltpu.make_async_remote_copy(
            fil.at[ROWS, pl.ds(c * CHUNK, CHUNK)],
            fil.at[0, pl.ds(c * CHUNK, CHUNK)],
            fs_send.at[c], fs_recv.at[c], next_il, MESH_ID,
        ))
        f_copies[c].start()
    loads[4].wait()

    def image_strip(i, jb, sums, scale=None):
        rows = pl.ds(pl.multiple_of(jb * 8, 8), 8)
        fx_here = fx[i, pl.ds(pl.multiple_of(jb * 8 + 8, 8), 8)]
        fx_behind = jnp.where(first_r, fx[i, pl.ds(jb * 8 + 7, 1)], pltpu.roll(fx_here, 1, 0))
        before = fil[i, rows]
        if scale is not None:
            before = scale * before
        here = u[i, rows]
        q = (before - fil[i + 1, rows]) + (fx_behind - fx_here) + diff_t(h[i, rows]) + damping * here
        image[i, rows] = q
        r = res[i, rows]
        rr, dq, rq, qq = sums
        return rr + r * r, dq + here * q, rq + r * q, qq + q * q

    sums = tuple(jnp.zeros((8, NT), F32) for _ in range(4))
    for i in range(1, ROWS):
        sums = lax.fori_loop(0, STRIPS, lambda jb, s, i=i: image_strip(i, jb, s), sums, unroll=True)
    for c in range(CHUNKS):
        f_copies[c].wait_recv()
        sums = lax.fori_loop(
            c * CHUNK // 8, (c + 1) * CHUNK // 8,
            lambda jb, s: image_strip(0, jb, s, had_il), sums, unroll=True)

    lane1 = lax.broadcasted_iota(jnp.int32, (8, 128), 1)
    row = jnp.zeros((8, 128), F32)
    for k, total in enumerate(sums):
        v = total[:, 0:128] + total[:, 128:256] + total[:, 256:384] + total[:, 384:512]
        v = v + pltpu.roll(v, 64, 1)
        v = v + pltpu.roll(v, 32, 1)
        row = jnp.where(lane1 // 32 == k, v, row)
    row = jnp.sum(row, axis=0, keepdims=True)

    for phase in range(3):
        msg[phase, 0:1] = row
        box[phase, 7:8] = row
        for d in order:
            pltpu.make_async_remote_copy(
                msg.at[phase, pl.ds(0, 1)], box.at[phase, pl.ds(d - 1, 1)],
                r_send.at[phase], r_recv.at[phase], peer(phase, d), MESH_ID,
            ).start()
        drain = pltpu.make_async_remote_copy(
            box.at[phase, pl.ds(0, 7)], box.at[phase, pl.ds(0, 7)],
            r_send.at[phase], r_recv.at[phase], peer(phase, 1), MESH_ID)
        drain.wait_recv()
        row = jnp.sum(box[phase], axis=0, keepdims=True)

    full = jnp.broadcast_to(row, (8, 128))
    rr, dq, rq, qq = (
        jnp.sum(jnp.where(lane1 // 32 == k, full, 0.0), axis=1, keepdims=True) for k in range(4))
    alpha = rr / dq
    beta = (rr - 2.0 * alpha * rq + alpha * alpha * qq) / rr
    coef[...] = jnp.where(lane1 == 0, alpha, beta)

    for copy in u_copies + f_copies:
        copy.wait_send()
    x_u.wait_send()
    x_f.wait_send()
    for phase in range(3):
        pltpu.make_async_remote_copy(
            box.at[phase, pl.ds(0, 7)], box.at[phase, pl.ds(0, 7)],
            r_send.at[phase], r_recv.at[phase], peer(phase, 1), MESH_ID).wait_send()


def apply(residual, direction, slope_il, slope_xl, weights):
    hbm, vmem = pl.BlockSpec(memory_space=pltpu.HBM), pl.BlockSpec(memory_space=pltpu.VMEM)
    block = (ROWS, COLS, NT)
    dma = pltpu.SemaphoreType.DMA
    return pl.pallas_call(
        kernel,
        out_shape=(jax.ShapeDtypeStruct(block, F32), jax.ShapeDtypeStruct((8, 128), F32)),
        in_specs=[hbm] * 5,
        out_specs=(vmem, vmem),
        scratch_shapes=[
            pltpu.VMEM(block, F32),
            pltpu.VMEM((ROWS + 1, COLS + 8, NT), F32),
            pltpu.VMEM(block, F32),
            pltpu.VMEM(block, F32),
            pltpu.VMEM(block, F32),
            pltpu.VMEM((ROWS + 1, COLS, NT), F32),
            pltpu.VMEM((ROWS, COLS + 8, NT), F32),
            pltpu.VMEM(block, F32),
            pltpu.VMEM((ROWS, NT), F32),
            pltpu.VMEM((ROWS, NT), F32),
            pltpu.VMEM((2 * ROWS, NT), F32),
            pltpu.VMEM((2 * ROWS, NT), F32),
            pltpu.VMEM((3, 8, 128), F32),
            pltpu.VMEM((3, 8, 128), F32),
            dma((5,)),
            dma((CHUNKS,)), dma((CHUNKS,)), dma((CHUNKS,)), dma((CHUNKS,)),
            dma((2,)), dma((2,)), dma((3,)), dma((3,)),
        ],
        compiler_params=pltpu.CompilerParams(
            collective_id=0, has_side_effects=True, vmem_limit_bytes=24 * 2**20),
    )(residual, direction, slope_il, slope_xl, weights)


def body(solution, residual, direction, slope_il, slope_xl, weights):
    image, coef = apply(residual, direction, slope_il, slope_xl, weights)
    alpha, beta = coef[0, 0], coef[0, 1]
    new_solution = solution + alpha * direction
    new_residual = residual - alpha * image
    new_direction = new_residual + beta * direction
    return new_solution, new_residual, new_direction


def solution(mesh):
    spec = P("il", "xl", None)
    return jax.shard_map(
        body, mesh=mesh, in_specs=(spec,) * 6, out_specs=(spec,) * 3, check_vma=False)
```

time: 86.1 us -> 46.1 us (0.54)
  blocking collectives: 59.2 us -> 0 us
  Pallas kernels: 0 us -> 36.5 us
  starting transfers between devices: 11.7 us -> 0 us
  between operations: 4.8 us -> 0.65 us
  local copies, waits for them, and re-layouts: 1.9 us -> 5.85 us
  waiting for transfers between devices: 3.66 us -> 0 us
  other arithmetic: 4.35 us -> 2.63 us
    psum x5 -> x0, blocking collectives: 59.2 us -> none  [over_axes(): value = lax.psum(value, axis)]
    pallas_call x0 -> x1, Pallas kernels: none -> 36.5 us  [apply(): pl.pallas_call(kernel, out_shape=(jax.ShapeDtypeStruct(block, F32), jax.S...]
    ppermute x4 -> x0, starting transfers between devices: 11.7 us -> none  [shifted(): return lax.ppermute(value, axis, pairs)]
    unnamed x10 -> x12, local copies, waits for them, and re-layouts: 0.03 us -> 5.2 us
    ppermute x4 -> x0, waiting for transfers between devices: 3.66 us -> none  [shifted(): return lax.ppermute(value, axis, pairs)]
    mul x1 -> x0, other arithmetic: 1.69 us -> none  [normal_apply(): term_il = behind_il - flux_il + time_diff(slope_il * flux_il)]
    reduce_sum x1 -> x0, other arithmetic: 1.3 us -> none  [body(): jnp.sum(image * image)]
    add x1, other arithmetic: 1.35 us -> 2.63 us  [body(): new_direction = new_residual + beta * direction]
  transfers between devices with their start and end apart: 4 -> 0, of which waited for: 3 -> 0; matrix products, arithmetic and copies ran while one was open for 1% -> 0% of each run, Pallas kernels for 0% -> 0%
where the time goes in v1:
time: 46.1 us; the launch traced here: 45.7 us
  Pallas kernels  36.5 us (79%)
  local copies, waits for them, and re-layouts  5.85 us (13%)
  other arithmetic  2.63 us (6%)
  between operations  0.65 us (1%)
    pallas_call x1, Pallas kernels, apply(): pl.pallas_call(kernel, out_shape=(jax.ShapeDtypeStruct(block, F32), jax.S...  36.5 us
    unnamed x12, local copies, waits for them, and re-layouts  5.2 us
    add x1, other arithmetic, body(): new_direction = new_residual + beta * direction  2.63 us

profile of v1, /device:TPU:8, one launch (start us, length us, event | category | flops | bytes accessed | tf_op | source)
XLA Modules:
  0.0 45.7 jit_solution(12303382255966546534)
XLA Ops:
  0.6 0.0 copy-start
  0.6 1.0 %copy-done = f32[4,64,512]{2,1,0:T(8,128)S(1)} copy-done((f32[4,64,512]{2,1,0:T(8,128)S(1)}, f32[4,64,512]{2,1,0:T(8,128)}, u32[]{:S(2)}) %copy-start) | copy-done | bytes 524312
  1.7 0.0 copy-start.1
  1.7 1.0 %copy-done.1 = f32[4,64,512]{2,1,0:T(8,128)S(1)} copy-done((f32[4,64,512]{2,1,0:T(8,128)S(1)}, f32[4,64,512]{2,1,0:T(8,128)}, u32[]{:S(2)}) %copy-start.1) | copy-done | bytes 524312
  2.7 0.0 copy-start.2
  2.7 1.0 %copy-done.2 = f32[4,64,512]{2,1,0:T(8,128)S(1)} copy-done((f32[4,64,512]{2,1,0:T(8,128)S(1)}, f32[4,64,512]{2,1,0:T(8,128)}, u32[]{:S(2)}) %copy-start.2) | copy-done | bytes 524312
  3.8 0.0 copy-start.3
  3.8 1.0 %copy-done.3 = f32[4,64,512]{2,1,0:T(8,128)S(1)} copy-done((f32[4,64,512]{2,1,0:T(8,128)S(1)}, f32[4,64,512]{2,1,0:T(8,128)}, u32[]{:S(2)}) %copy-start.3) | copy-done | bytes 524312
  4.8 0.0 copy-start.4
  4.8 1.0 %copy-done.4 = f32[4,64,512]{2,1,0:T(8,128)S(1)} copy-done((f32[4,64,512]{2,1,0:T(8,128)S(1)}, f32[4,64,512]{2,1,0:T(8,128)}, u32[]{:S(2)}) %copy-start.4) | copy-done | bytes 524312
  5.8 0.0 copy-start.5
  5.8 36.5 %shard_map.85 = (f32[4,64,512]{2,1,0:T(8,128)S(1)}, f32[8,128]{1,0:T(8,128)S(1)}) custom-call(f32[4,64,512]{2,1,0:T(8,128)S(1)} %copy-done.1, f32[4,64,512]{2,1,0:T(8,128)S(1)} %copy-done, f32[4,64,512]{2,1,0:T(8,128)S(1)} %copy-done.2, f32[4,64,512]{2,1,0:T(8,128)S(1)} %copy-done.3, f32[4,64,512]{2,1,0:T(8,128)S(1)} %copy-done.4), custom_call_target="tpu_custom_call" | custom-call | tf_op jit(solution)/shard_map/pallas_call | solution.py:228
  42.4 0.7 %fusion = (f32[1,1]{1,0:T(1,128)}, f32[1,1]{1,0:T(1,128)}) fusion(f32[8,128]{1,0:T(8,128)S(1)} %get-tuple-element.5), kind=kLoop, calls=%fused_computation.3 | loop fusion | bytes 16 | tf_op jit(solution)/shard_map/slice | solution.py:259
  43.1 0.0 copy-done.5
  43.1 2.6 %multiply_add_fusion = (f32[4,64,512]{2,1,0:T(8,128)}, f32[4,64,512]{2,1,0:T(8,128)}, f32[4,64,512]{2,1,0:T(8,128)}) fusion(f32[4,64,512]{2,1,0:T(8,128)S(1)} %copy-done, f32[]{:T(128)} %bitcast.1, f32[4,64,512]{2,1,0:T(8,128)S(1)} %copy-done.1, f32[4,64,512]{2,1,0:T(8,128)S(1)} %get-tuple-element.6, f32[]{:T(128)} %bitcast, f32[4,64,512]{2,1,0:T(8,128)S(1)} %copy-done.5), kind=kLoop, calls=%fused_computation | loop fusion | flops 786432 | bytes 3670024 | tf_op jit(solution)/shard_map/add | solution.py:262
Async XLA Ops:
  0.6 1.0 %copy-start = (f32[4,64,512]{2,1,0:T(8,128)S(1)}, f32[4,64,512]{2,1,0:T(8,128)}, u32[]{:S(2)}) copy-start(f32[4,64,512]{2,1,0:T(8,128)} %u_hbm.1) | copy-start | bytes 1572868
  1.7 1.0 %copy-start.1 = (f32[4,64,512]{2,1,0:T(8,128)S(1)}, f32[4,64,512]{2,1,0:T(8,128)}, u32[]{:S(2)}) copy-start(f32[4,64,512]{2,1,0:T(8,128)} %res_hbm.1) | copy-start | bytes 1572868
  2.7 1.0 %copy-start.2 = (f32[4,64,512]{2,1,0:T(8,128)S(1)}, f32[4,64,512]{2,1,0:T(8,128)}, u32[]{:S(2)}) copy-start(f32[4,64,512]{2,1,0:T(8,128)} %sil_hbm.1) | copy-start | bytes 1572868
  3.8 1.0 %copy-start.3 = (f32[4,64,512]{2,1,0:T(8,128)S(1)}, f32[4,64,512]{2,1,0:T(8,128)}, u32[]{:S(2)}) copy-start(f32[4,64,512]{2,1,0:T(8,128)} %sxl_hbm.1) | copy-start | bytes 1572868
  4.8 1.0 %copy-start.4 = (f32[4,64,512]{2,1,0:T(8,128)S(1)}, f32[4,64,512]{2,1,0:T(8,128)}, u32[]{:S(2)}) copy-start(f32[4,64,512]{2,1,0:T(8,128)} %w_hbm.1) | copy-start | bytes 1572868
  5.8 37.2 %copy-start.5 = (f32[4,64,512]{2,1,0:T(8,128)S(1)}, f32[4,64,512]{2,1,0:T(8,128)}, u32[]{:S(2)}) copy-start(f32[4,64,512]{2,1,0:T(8,128)} %param.6) | copy-start | bytes 1572868

commit v2 on v1

v2 whole, which is shorter than its diff:
```python
import jax
import jax.numpy as jnp
from jax import lax
from jax.experimental import pallas as pl
from jax.experimental.pallas import tpu as pltpu
from jax.sharding import PartitionSpec as P

damping = 0.3
F32 = jnp.float32
MESH_ID = pl.DeviceIdType.MESH

NIL, NXL = 64, 8
ROWS, COLS, NT = 4, 64, 512
STRIPS = COLS // 8


def kernel(
    sol_hbm, res_hbm, u_hbm, sil_hbm, sxl_hbm, w_hbm,
    sol, res, u, image, coef,
    sil, sxl, w, fil, fx, h, u_in, w_in, g_out, g_in, xl_u_out, xl_u_in, xl_f_out, xl_f_in,
    msg, box,
    load_sem, i_send, i_recv, x_send, x_recv, r_send, r_recv,
):
    il, xl = lax.axis_index("il"), lax.axis_index("xl")
    z_hi, y, core = il // 16, (il // 2) % 8, il % 2
    z_lo, x = xl // 4, xl % 4
    next_il = ((il + 1) % NIL, xl)
    prev_il = ((il + NIL - 1) % NIL, xl)
    next_xl = (il, (xl + 1) % NXL)
    prev_xl = (il, (xl + NXL - 1) % NXL)
    near = x * 2 + core
    z = z_hi * 2 + z_lo

    def peer(phase, d):
        if phase == 0:
            k = (near + d) % 8
            return (il - core + k % 2, z_lo * 4 + k // 2)
        if phase == 1:
            return (z_hi * 16 + ((y + d) % 8) * 2 + core, xl)
        k = (z + d) % 8
        return ((k // 2) * 16 + y * 2 + core, (k % 2) * 4 + x)

    order = (4, 3, 5, 2, 6, 1, 7)
    barrier = pltpu.get_barrier_semaphore()
    peers = [next_il, prev_il, next_xl, prev_xl]
    peers += [peer(phase, d) for phase in (2, 1, 0) for d in order]
    for other in peers:
        pl.semaphore_signal(barrier, inc=1, device_id=other, device_id_type=MESH_ID)

    loads = [
        pltpu.make_async_copy(source, target, load_sem.at[k])
        for k, (source, target) in enumerate((
            (u_hbm, u), (sil_hbm, sil), (w_hbm, w), (sxl_hbm, sxl), (res_hbm, res), (sol_hbm, sol)))
    ]
    for load in loads:
        load.start()
    pl.semaphore_wait(barrier, len(peers))

    i_u = pltpu.make_async_remote_copy(
        u_hbm.at[0], u_in, i_send.at[0], i_recv.at[0], prev_il, MESH_ID)
    i_u.start()
    i_w = pltpu.make_async_remote_copy(
        w_hbm.at[ROWS - 1], w_in, i_send.at[1], i_recv.at[1], next_il, MESH_ID)
    i_w.start()

    lane = lax.broadcasted_iota(jnp.int32, (8, NT), 1)
    sub = lax.broadcasted_iota(jnp.int32, (8, NT), 0)
    first_t, last_t = lane == 0, lane == NT - 1
    first_r, last_r = sub == 0, sub == 7

    def diff_t(v):
        ahead = jnp.where(last_t, 0.0, pltpu.roll(v, NT - 1, 1))
        behind = jnp.where(first_t, 0.0, pltpu.roll(v, 1, 1))
        return 0.5 * (ahead - behind)

    loads[0].wait()
    loads[1].wait()

    def lean(jb, _):
        rows = pl.ds(pl.multiple_of(jb * 8, 8), 8)
        here = u[ROWS - 1, rows]
        g_out[rows] = here + sil[ROWS - 1, rows] * diff_t(here)
        return 0
    lax.fori_loop(0, STRIPS, lean, 0, unroll=True)
    i_g = pltpu.make_async_remote_copy(g_out, g_in, i_send.at[2], i_recv.at[2], next_il, MESH_ID)
    i_g.start()

    for i in range(ROWS):
        xl_u_out[i:i + 1] = u[i, 0:1]
    x_u = pltpu.make_async_remote_copy(
        xl_u_out, xl_u_in, x_send.at[0], x_recv.at[0], prev_xl, MESH_ID)
    x_u.start()
    loads[2].wait()
    loads[3].wait()
    for i in range(ROWS):
        tail = slice(COLS - 8, COLS)
        g = u[i, tail] + sxl[i, tail] * diff_t(u[i, tail])
        xl_f_out[i:i + 1] = g[7:8]
        xl_f_out[ROWS + i:ROWS + i + 1] = w[i, tail][7:8]
    x_f = pltpu.make_async_remote_copy(
        xl_f_out, xl_f_in, x_send.at[1], x_recv.at[1], next_xl, MESH_ID)
    x_f.start()

    keep_il = jnp.where(il == NIL - 1, 0.0, 1.0).astype(F32)
    keep_xl = jnp.where(xl == NXL - 1, 0.0, 1.0).astype(F32)
    had_il = jnp.where(il == 0, 0.0, 1.0).astype(F32)
    had_xl = jnp.where(xl == 0, 0.0, 1.0).astype(F32)

    def put_strip(i, jb, next_row, last=False):
        start = pl.multiple_of(jb * 8, 8)
        rows = pl.ds(start, 8)
        here = u[i, rows]
        t = diff_t(here)
        wt = w[i, rows]
        sq = wt * wt
        ahead = jnp.where(last_r, next_row, pltpu.roll(here, 7, 0))
        slope = sxl[i, rows]
        flux = sq * (ahead - here - slope * t)
        if last:
            flux = jnp.where(last_r, keep_xl * flux, flux)
        fx[i, pl.ds(start + 8, 8)] = flux
        part = slope * flux
        if i < ROWS - 1:
            slope = sil[i, rows]
            f = sq * (u[i + 1, rows] - here - slope * t)
            fil[i, rows] = f
            part = part + slope * f
        h[i, rows] = part

    for i in range(ROWS):
        def strip(jb, _, i=i):
            put_strip(i, jb, u[i, pl.ds(jb * 8 + 8, 1)])
            return 0
        lax.fori_loop(0, STRIPS - 1, strip, 0, unroll=True)

    x_u.wait_recv()
    for i in range(ROWS):
        put_strip(i, STRIPS - 1, xl_u_in[i:i + 1], True)
    x_f.wait_recv()
    for i in range(ROWS):
        wt = xl_f_in[ROWS + i:ROWS + i + 1]
        fx[i, 7:8] = had_xl * (wt * wt * (u[i, 0:1] - xl_f_in[i:i + 1]))
    loads[4].wait()

    def image_strip(i, jb, sums):
        rows = pl.ds(pl.multiple_of(jb * 8, 8), 8)
        fx_here = fx[i, pl.ds(pl.multiple_of(jb * 8 + 8, 8), 8)]
        fx_behind = jnp.where(first_r, fx[i, pl.ds(jb * 8 + 7, 1)], pltpu.roll(fx_here, 1, 0))
        here = u[i, rows]
        if i == 0:
            wt = w_in[rows]
            before = had_il * (wt * wt * (here - g_in[rows]))
        else:
            before = fil[i - 1, rows]
        q = (before - fil[i, rows]) + (fx_behind - fx_here) + diff_t(h[i, rows]) + damping * here
        image[i, rows] = q
        r = res[i, rows]
        rr, dq, rq, qq = sums
        return rr + r * r, dq + here * q, rq + r * q, qq + q * q

    def image_inline(i, sums):
        return lax.fori_loop(0, STRIPS, lambda jb, s: image_strip(i, jb, s), sums, unroll=True)

    sums = tuple(jnp.zeros((8, NT), F32) for _ in range(4))
    for i in range(1, ROWS - 1):
        sums = image_inline(i, sums)

    i_u.wait_recv()

    def last_inline(jb, _):
        rows = pl.ds(pl.multiple_of(jb * 8, 8), 8)
        wt = w[ROWS - 1, rows]
        f = keep_il * (wt * wt * (u_in[rows] - g_out[rows]))
        fil[ROWS - 1, rows] = f
        h[ROWS - 1, rows] = h[ROWS - 1, rows] + sil[ROWS - 1, rows] * f
        return 0
    lax.fori_loop(0, STRIPS, last_inline, 0, unroll=True)
    sums = image_inline(ROWS - 1, sums)

    i_w.wait_recv()
    i_g.wait_recv()
    sums = image_inline(0, sums)

    lane1 = lax.broadcasted_iota(jnp.int32, (8, 128), 1)
    row = jnp.zeros((8, 128), F32)
    for k, total in enumerate(sums):
        v = total[:, 0:128] + total[:, 128:256] + total[:, 256:384] + total[:, 384:512]
        v = v + pltpu.roll(v, 64, 1)
        v = v + pltpu.roll(v, 32, 1)
        row = jnp.where(lane1 // 32 == k, v, row)
    row = jnp.sum(row, axis=0, keepdims=True)

    for phase in range(3):
        msg[phase, 0:1] = row
        box[phase, 7:8] = row
        for d in order:
            pltpu.make_async_remote_copy(
                msg.at[phase, pl.ds(0, 1)], box.at[phase, pl.ds(d - 1, 1)],
                r_send.at[phase], r_recv.at[phase], peer(phase, d), MESH_ID,
            ).start()
        drain = pltpu.make_async_remote_copy(
            box.at[phase, pl.ds(0, 7)], box.at[phase, pl.ds(0, 7)],
            r_send.at[phase], r_recv.at[phase], peer(phase, 1), MESH_ID)
        drain.wait_recv()
        row = jnp.sum(box[phase], axis=0, keepdims=True)

    full = jnp.broadcast_to(row, (8, 128))
    rr, dq, rq, qq = (
        jnp.sum(jnp.where(lane1 // 32 == k, full, 0.0), axis=1, keepdims=True) for k in range(4))
    alpha = rr / dq
    beta = (rr - 2.0 * alpha * rq + alpha * alpha * qq) / rr
    coef[...] = jnp.where(lax.broadcasted_iota(jnp.int32, (8, 128), 0) == 0, alpha, beta)

    for copy in (i_u, i_w, i_g, x_u, x_f):
        copy.wait_send()
    for phase in range(3):
        pltpu.make_async_remote_copy(
            box.at[phase, pl.ds(0, 7)], box.at[phase, pl.ds(0, 7)],
            r_send.at[phase], r_recv.at[phase], peer(phase, 1), MESH_ID).wait_send()
    loads[5].wait()


def apply(solution, residual, direction, slope_il, slope_xl, weights):
    hbm, vmem = pl.BlockSpec(memory_space=pltpu.HBM), pl.BlockSpec(memory_space=pltpu.VMEM)
    block, plane, line = (ROWS, COLS, NT), (COLS, NT), (ROWS, NT)
    dma = pltpu.SemaphoreType.DMA
    operands = (
        pltpu.with_memory_space_constraint(v, pltpu.HBM)
        for v in (solution, residual, direction, slope_il, slope_xl, weights))
    return pl.pallas_call(
        kernel,
        out_shape=(jax.ShapeDtypeStruct(block, F32),) * 4 + (jax.ShapeDtypeStruct((8, 128), F32),),
        in_specs=[hbm] * 6,
        out_specs=(vmem,) * 5,
        scratch_shapes=[
            pltpu.VMEM(shape, F32)
            for shape in (
                block, block, block, block, (ROWS, COLS + 8, NT), block, plane, plane, plane, plane,
                line, line, (2 * ROWS, NT), (2 * ROWS, NT), (3, 8, 128), (3, 8, 128))
        ] + [dma((6,)), dma((3,)), dma((3,)), dma((2,)), dma((2,)), dma((3,)), dma((3,))],
        compiler_params=pltpu.CompilerParams(
            collective_id=0, has_side_effects=True, vmem_limit_bytes=24 * 2**20),
    )(*operands)


def update_kernel(sol, res, u, image, coef, new_sol_hbm, new_res_hbm, new_dir_hbm, outs, sems):
    alpha = jnp.broadcast_to(coef[0:1, 0:128], (8, 128))
    beta = jnp.broadcast_to(coef[1:2, 0:128], (8, 128))
    alpha = jnp.concatenate([alpha] * (NT // 128), axis=1)
    beta = jnp.concatenate([beta] * (NT // 128), axis=1)
    copies = []
    for i in range(ROWS):
        def strip(jb, _, i=i):
            rows = pl.ds(pl.multiple_of(jb * 8, 8), 8)
            here = u[i, rows]
            r = res[i, rows] - alpha * image[i, rows]
            outs[0, i, rows] = sol[i, rows] + alpha * here
            outs[1, i, rows] = r
            outs[2, i, rows] = r + beta * here
            return 0
        lax.fori_loop(0, STRIPS, strip, 0, unroll=True)
        for k, target in enumerate((new_sol_hbm, new_res_hbm, new_dir_hbm)):
            copies.append(pltpu.make_async_copy(outs.at[k, i], target.at[i], sems.at[k, i]))
            copies[-1].start()
    for copy in copies:
        copy.wait()


def update(sol, res, u, image, coef):
    hbm, vmem = pl.BlockSpec(memory_space=pl.ANY), pl.BlockSpec(memory_space=pltpu.VMEM)
    block = (ROWS, COLS, NT)
    return pl.pallas_call(
        update_kernel,
        out_shape=(jax.ShapeDtypeStruct(block, F32),) * 3,
        in_specs=[vmem] * 5,
        out_specs=(hbm,) * 3,
        scratch_shapes=[pltpu.VMEM((3,) + block, F32), pltpu.SemaphoreType.DMA((3, ROWS))],
        compiler_params=pltpu.CompilerParams(vmem_limit_bytes=8 * 2**20),
    )(sol, res, u, image, coef)


def body(solution, residual, direction, slope_il, slope_xl, weights):
    return update(*apply(solution, residual, direction, slope_il, slope_xl, weights))


def solution(mesh):
    spec = P("il", "xl", None)
    return jax.shard_map(
        body, mesh=mesh, in_specs=(spec,) * 6, out_specs=(spec,) * 3, check_vma=False)
```

time: 46.1 us -> 35.7 us (0.77)
  local copies, waits for them, and re-layouts: 5.85 us -> 0 us
  other arithmetic: 2.63 us -> 0 us
  Pallas kernels: 36.5 us -> 34.9 us
    unnamed x12 -> x0, local copies, waits for them, and re-layouts: 5.2 us -> none
    add x1 -> x0, other arithmetic: 2.63 us -> none  [body(): new_direction = new_residual + beta * direction]
    pallas_call x1 -> x2, Pallas kernels: 36.5 us -> 34.9 us  [the longest x1 33.7 us: apply(): pl.pallas_call(kernel, out_shape=(jax.ShapeDtypeStruct(block, F32),) * 4...]
    slice x1 -> x0, local copies, waits for them, and re-layouts: 0.65 us -> none  [body(): alpha, beta = (coef[0, 0], coef[0, 1])]
where the time goes in v2:
time: 35.7 us; the launch traced here: 35.6 us
  Pallas kernels  34.9 us (98%)
  between operations  0.64 us (2%)
    pallas_call x1, Pallas kernels, apply(): pl.pallas_call(kernel, out_shape=(jax.ShapeDtypeStruct(block, F32),) * 4...  33.7 us
    pallas_call x1, Pallas kernels, update(): pl.pallas_call(update_kernel, out_shape=(jax.ShapeDtypeStruct(block, F32)...  1.27 us

profile of v2, /device:TPU:8, one launch (start us, length us, event | category | flops | bytes accessed | tf_op | source)
XLA Modules:
  0.0 35.6 jit_solution(12534800468873087504)
XLA Ops:
  0.6 33.7 %shard_map.85 = (f32[4,64,512]{2,1,0:T(8,128)S(1)}, f32[4,64,512]{2,1,0:T(8,128)S(1)}, f32[4,64,512]{2,1,0:T(8,128)S(1)}, f32[4,64,512]{2,1,0:T(8,128)S(1)}, f32[8,128]{1,0:T(8,128)S(1)}) custom-call(f32[4,64,512]{2,1,0:T(8,128)} %sol_hbm.1, f32[4,64,512]{2,1,0:T(8,128)} %res_hbm.1, f32[4,64,512]{2,1,0:T(8,128)} %u_hbm.1, f32[4,64,512]{2,1,0:T(8,128)} %sil_hbm.1, ...), custom_call_target="tpu_custom_call" | custom-call | tf_op jit(solution)/shard_map/pallas_call | solution.py:230
  34.3 1.3 %shard_map.86 = (f32[4,64,512]{2,1,0:T(8,128)}, f32[4,64,512]{2,1,0:T(8,128)}, f32[4,64,512]{2,1,0:T(8,128)}) custom-call(f32[4,64,512]{2,1,0:T(8,128)S(1)} %get-tuple-element.8.sol, f32[4,64,512]{2,1,0:T(8,128)S(1)} %get-tuple-element.9.res, f32[4,64,512]{2,1,0:T(8,128)S(1)} %get-tuple-element.10.u, f32[4,64,512]{2,1,0:T(8,128)S(1)} %get-tuple-element.11.image, ...), custom_call_target="tpu_custom_call" | custom-call | tf_op jit(solution)/shard_map/pallas_call | solution.py:272

commit v3 on v2

--- a/solution.py
+++ b/solution.py
@@ -18,34 +18,41 @@
     sol_hbm, res_hbm, u_hbm, sil_hbm, sxl_hbm, w_hbm,
     sol, res, u, image, coef,
     sil, sxl, w, fil, fx, h, u_in, w_in, g_out, g_in, xl_u_out, xl_u_in, xl_f_out, xl_f_in,
-    msg, box,
-    load_sem, i_send, i_recv, x_send, x_recv, r_send, r_recv,
+    msg, box_xy, box_zc,
+    load_sem, i_send, i_recv, x_send, x_recv, r_send, r_recv, go,
 ):
     il, xl = lax.axis_index("il"), lax.axis_index("xl")
     z_hi, y, core = il // 16, (il // 2) % 8, il % 2
     z_lo, x = xl // 4, xl % 4
-    next_il = ((il + 1) % NIL, xl)
-    prev_il = ((il + NIL - 1) % NIL, xl)
-    next_xl = (il, (xl + 1) % NXL)
-    prev_xl = (il, (xl + NXL - 1) % NXL)
-    near = x * 2 + core
     z = z_hi * 2 + z_lo
 
-    def peer(phase, d):
-        if phase == 0:
-            k = (near + d) % 8
-            return (il - core + k % 2, z_lo * 4 + k // 2)
-        if phase == 1:
-            return (z_hi * 16 + ((y + d) % 8) * 2 + core, xl)
-        k = (z + d) % 8
-        return ((k // 2) * 16 + y * 2 + core, (k % 2) * 4 + x)
-
-    order = (4, 3, 5, 2, 6, 1, 7)
+    def at(dx=0, dy=0, dz=0, dc=0):
+        nz = (z + dz) % 8
+        return ((nz // 2) * 16 + ((y + dy) % 8) * 2 + (core + dc) % 2, (nz % 2) * 4 + (x + dx) % 4)
+
+    def along(il_by, xl_by=0):
+        return ((il + il_by + NIL) % NIL, (xl + xl_by + NXL) % NXL)
+
+    next_il, prev_il, next_xl, prev_xl = along(1), along(-1), along(0, 1), along(0, -1)
+    sibling = at(dc=1)
+
     barrier = pltpu.get_barrier_semaphore()
-    peers = [next_il, prev_il, next_xl, prev_xl]
-    peers += [peer(phase, d) for phase in (2, 1, 0) for d in order]
+    neighbours = [at(dx=1), at(dx=3), at(dy=1), at(dy=7), at(dz=1), at(dz=7)]
+    peers = [next_il, prev_il, along(2), along(-2), next_xl, prev_xl] + neighbours
+    steps = (
+        neighbours,
+        [at(dy=2), at(dy=6), at(dz=2), at(dz=6)],
+        [at(dx=1), at(dx=2), at(dx=3), sibling],
+    )
     for other in peers:
         pl.semaphore_signal(barrier, inc=1, device_id=other, device_id_type=MESH_ID)
+
+    def say(step):
+        for other in steps[step]:
+            pl.semaphore_signal(go.at[step], inc=1, device_id=other, device_id_type=MESH_ID)
+
+    def hear(step):
+        pl.semaphore_wait(go.at[step], len(steps[step]))
 
     loads = [
         pltpu.make_async_copy(source, target, load_sem.at[k])
@@ -60,8 +67,11 @@
         u_hbm.at[0], u_in, i_send.at[0], i_recv.at[0], prev_il, MESH_ID)
     i_u.start()
     i_w = pltpu.make_async_remote_copy(
-        w_hbm.at[ROWS - 1], w_in, i_send.at[1], i_recv.at[1], next_il, MESH_ID)
+        w_hbm.at[ROWS - 1], w_in.at[1], i_send.at[1], i_recv.at[1], sibling, MESH_ID)
     i_w.start()
+    relay = pltpu.make_async_remote_copy(
+        w_in.at[1], w_in.at[0], i_send.at[3], i_recv.at[3], along(2), MESH_ID)
+    say(0)
 
     lane = lax.broadcasted_iota(jnp.int32, (8, NT), 1)
     sub = lax.broadcasted_iota(jnp.int32, (8, NT), 0)
@@ -85,6 +95,12 @@
     i_g = pltpu.make_async_remote_copy(g_out, g_in, i_send.at[2], i_recv.at[2], next_il, MESH_ID)
     i_g.start()
 
+    @pl.when(core == 0)
+    def _():
+        i_w.wait_recv()
+        relay.start()
+
+
     for i in range(ROWS):
         xl_u_out[i:i + 1] = u[i, 0:1]
     x_u = pltpu.make_async_remote_copy(
@@ -100,6 +116,8 @@
     x_f = pltpu.make_async_remote_copy(
         xl_f_out, xl_f_in, x_send.at[1], x_recv.at[1], next_xl, MESH_ID)
     x_f.start()
+    hear(0)
+    say(1)
 
     keep_il = jnp.where(il == NIL - 1, 0.0, 1.0).astype(F32)
     keep_xl = jnp.where(xl == NXL - 1, 0.0, 1.0).astype(F32)
@@ -133,6 +151,9 @@
             return 0
         lax.fori_loop(0, STRIPS - 1, strip, 0, unroll=True)
 
+    hear(1)
+    say(2)
+
     x_u.wait_recv()
     for i in range(ROWS):
         put_strip(i, STRIPS - 1, xl_u_in[i:i + 1], True)
@@ -148,7 +169,7 @@
         fx_behind = jnp.where(first_r, fx[i, pl.ds(jb * 8 + 7, 1)], pltpu.roll(fx_here, 1, 0))
         here = u[i, rows]
         if i == 0:
-            wt = w_in[rows]
+            wt = w_in[core, rows]
             before = had_il * (wt * wt * (here - g_in[rows]))
         else:
             before = fil[i - 1, rows]
@@ -177,9 +198,17 @@
     lax.fori_loop(0, STRIPS, last_inline, 0, unroll=True)
     sums = image_inline(ROWS - 1, sums)
 
-    i_w.wait_recv()
+    @pl.when(core == 0)
+    def _():
+        relay.wait_recv()
+
+    @pl.when(core == 1)
+    def _():
+        i_w.wait_recv()
+
     i_g.wait_recv()
     sums = image_inline(0, sums)
+    hear(2)
 
     lane1 = lax.broadcasted_iota(jnp.int32, (8, 128), 1)
     row = jnp.zeros((8, 128), F32)
@@ -190,19 +219,26 @@
         row = jnp.where(lane1 // 32 == k, v, row)
     row = jnp.sum(row, axis=0, keepdims=True)
 
-    for phase in range(3):
+    near = lambda by, size: min(by, size - by)
+    plane = [(dx, dy, 0, 0) for dx in range(4) for dy in range(8) if dx + dy > 0]
+    plane.sort(key=lambda p: -near(p[0], 4) - near(p[1], 8))
+    line = [(0, 0, dz, dc) for dz in range(8) for dc in range(2) if dz + dc > 0]
+    line.sort(key=lambda p: -near(p[2], 8))
+    drains = []
+    for phase, (offsets, box) in enumerate(((plane, box_xy), (line, box_zc))):
+        count = len(offsets)
         msg[phase, 0:1] = row
-        box[phase, 7:8] = row
-        for d in order:
+        box[count:count + 1] = row
+        for slot, by in enumerate(offsets):
             pltpu.make_async_remote_copy(
-                msg.at[phase, pl.ds(0, 1)], box.at[phase, pl.ds(d - 1, 1)],
-                r_send.at[phase], r_recv.at[phase], peer(phase, d), MESH_ID,
+                msg.at[phase, pl.ds(0, 1)], box.at[pl.ds(slot, 1)],
+                r_send.at[phase], r_recv.at[phase], at(*by), MESH_ID,
             ).start()
-        drain = pltpu.make_async_remote_copy(
-            box.at[phase, pl.ds(0, 7)], box.at[phase, pl.ds(0, 7)],
-            r_send.at[phase], r_recv.at[phase], peer(phase, 1), MESH_ID)
-        drain.wait_recv()
-        row = jnp.sum(box[phase], axis=0, keepdims=True)
+        drains.append(pltpu.make_async_remote_copy(
+            box.at[pl.ds(0, count)], box.at[pl.ds(0, count)],
+            r_send.at[phase], r_recv.at[phase], sibling, MESH_ID))
+        drains[phase].wait_recv()
+        row = jnp.sum(box[...], axis=0, keepdims=True)
 
     full = jnp.broadcast_to(row, (8, 128))
     rr, dq, rq, qq = (
@@ -213,10 +249,13 @@
 
     for copy in (i_u, i_w, i_g, x_u, x_f):
         copy.wait_send()
-    for phase in range(3):
-        pltpu.make_async_remote_copy(
-            box.at[phase, pl.ds(0, 7)], box.at[phase, pl.ds(0, 7)],
-            r_send.at[phase], r_recv.at[phase], peer(phase, 1), MESH_ID).wait_send()
+
+    @pl.when(core == 0)
+    def _():
+        relay.wait_send()
+
+    for drain in drains:
+        drain.wait_send()
     loads[5].wait()
 
 
@@ -235,9 +274,11 @@
         scratch_shapes=[
             pltpu.VMEM(shape, F32)
             for shape in (
-                block, block, block, block, (ROWS, COLS + 8, NT), block, plane, plane, plane, plane,
-                line, line, (2 * ROWS, NT), (2 * ROWS, NT), (3, 8, 128), (3, 8, 128))
-        ] + [dma((6,)), dma((3,)), dma((3,)), dma((2,)), dma((2,)), dma((3,)), dma((3,))],
+                block, block, block, block, (ROWS, COLS + 8, NT), block, plane, (2,) + plane, plane, plane,
+                line, line, (2 * ROWS, NT), (2 * ROWS, NT), (2, 8, 128), (32, 128), (16, 128))
+        ] + [
+            dma((6,)), dma((4,)), dma((4,)), dma((2,)), dma((2,)), dma((2,)), dma((2,)),
+            pltpu.SemaphoreType.REGULAR((3,))],
         compiler_params=pltpu.CompilerParams(
             collective_id=0, has_side_effects=True, vmem_limit_bytes=24 * 2**20),
     )(*operands)

time: 35.7 us -> 32.5 us (0.910)
  the two profiles are of different devices: /device:TPU:8 before, /device:TPU:1 now
where the time goes in v3:
time: 32.5 us; the launch traced here: 32.4 us
  Pallas kernels  31.7 us (98%)
  between operations  0.64 us (2%)
    pallas_call x1, Pallas kernels, apply(): pl.pallas_call(kernel, out_shape=(jax.ShapeDtypeStruct(block, F32),) * 4...  30.5 us
    pallas_call x1, Pallas kernels, update(): pl.pallas_call(update_kernel, out_shape=(jax.ShapeDtypeStruct(block, F32)...  1.27 us

profile of v3, /device:TPU:1, one launch (start us, length us, event | category | flops | bytes accessed | tf_op | source)
XLA Modules:
  0.0 32.4 jit_solution(7465592438243765318)
XLA Ops:
  0.6 30.5 %shard_map.85 = (f32[4,64,512]{2,1,0:T(8,128)S(1)}, f32[4,64,512]{2,1,0:T(8,128)S(1)}, f32[4,64,512]{2,1,0:T(8,128)S(1)}, f32[4,64,512]{2,1,0:T(8,128)S(1)}, f32[8,128]{1,0:T(8,128)S(1)}) custom-call(f32[4,64,512]{2,1,0:T(8,128)} %sol_hbm.1, f32[4,64,512]{2,1,0:T(8,128)} %res_hbm.1, f32[4,64,512]{2,1,0:T(8,128)} %u_hbm.1, f32[4,64,512]{2,1,0:T(8,128)} %sil_hbm.1, ...), custom_call_target="tpu_custom_call" | custom-call | tf_op jit(solution)/shard_map/pallas_call | solution.py:269
  31.1 1.3 %shard_map.86 = (f32[4,64,512]{2,1,0:T(8,128)}, f32[4,64,512]{2,1,0:T(8,128)}, f32[4,64,512]{2,1,0:T(8,128)}) custom-call(f32[4,64,512]{2,1,0:T(8,128)S(1)} %get-tuple-element.8.sol, f32[4,64,512]{2,1,0:T(8,128)S(1)} %get-tuple-element.9.res, f32[4,64,512]{2,1,0:T(8,128)S(1)} %get-tuple-element.10.u, f32[4,64,512]{2,1,0:T(8,128)S(1)} %get-tuple-element.11.image, ...), custom_call_target="tpu_custom_call" | custom-call | tf_op jit(solution)/shard_map/pallas_call | solution.py:313

commit v4 on v3

--- a/solution.py
+++ b/solution.py
@@ -30,21 +30,25 @@
         nz = (z + dz) % 8
         return ((nz // 2) * 16 + ((y + dy) % 8) * 2 + (core + dc) % 2, (nz % 2) * 4 + (x + dx) % 4)
 
-    def along(il_by, xl_by=0):
-        return ((il + il_by + NIL) % NIL, (xl + xl_by + NXL) % NXL)
-
-    next_il, prev_il, next_xl, prev_xl = along(1), along(-1), along(0, 1), along(0, -1)
+    next_il, prev_il = ((il + 1) % NIL, xl), ((il + NIL - 1) % NIL, xl)
+    next_xl, prev_xl = (il, (xl + 1) % NXL), (il, (xl + NXL - 1) % NXL)
+    has_next_il, has_prev_il = il < NIL - 1, il > 0
+    has_next_xl, has_prev_xl = xl < NXL - 1, xl > 0
     sibling = at(dc=1)
 
     barrier = pltpu.get_barrier_semaphore()
-    neighbours = [at(dx=1), at(dx=3), at(dy=1), at(dy=7), at(dz=1), at(dz=7)]
-    peers = [next_il, prev_il, along(2), along(-2), next_xl, prev_xl] + neighbours
+    flat, deep = [at(dx=1), at(dx=3), at(dy=1), at(dy=7)], [at(dz=1), at(dz=7)]
+    mesh_peers = (
+        (has_next_il, next_il), (has_prev_il, prev_il), (has_next_xl, next_xl), (has_prev_xl, prev_xl))
     steps = (
-        neighbours,
-        [at(dy=2), at(dy=6), at(dz=2), at(dz=6)],
-        [at(dx=1), at(dx=2), at(dx=3), sibling],
+        flat, [at(dy=2), at(dy=6)], [at(dx=1), at(dx=2), at(dx=3)],
+        deep, [at(dz=2), at(dz=6)], [sibling],
     )
-    for other in peers:
+    for has, other in mesh_peers:
+        @pl.when(has)
+        def _(other=other):
+            pl.semaphore_signal(barrier, inc=1, device_id=other, device_id_type=MESH_ID)
+    for other in flat + deep:
         pl.semaphore_signal(barrier, inc=1, device_id=other, device_id_type=MESH_ID)
 
     def say(step):
@@ -57,21 +61,28 @@
     loads = [
         pltpu.make_async_copy(source, target, load_sem.at[k])
         for k, (source, target) in enumerate((
-            (u_hbm, u), (sil_hbm, sil), (w_hbm, w), (sxl_hbm, sxl), (res_hbm, res), (sol_hbm, sol)))
+            (u_hbm, u), (w_hbm, w), (sil_hbm, sil), (sxl_hbm, sxl), (res_hbm, res), (sol_hbm, sol)))
     ]
-    for load in loads:
+    for load in loads[:4]:
         load.start()
-    pl.semaphore_wait(barrier, len(peers))
+    count = len(flat + deep)
+    for has, _ in mesh_peers:
+        count = count + has.astype(jnp.int32)
+    pl.semaphore_wait(barrier, count)
+    say(0)
+    say(3)
 
     i_u = pltpu.make_async_remote_copy(
         u_hbm.at[0], u_in, i_send.at[0], i_recv.at[0], prev_il, MESH_ID)
-    i_u.start()
     i_w = pltpu.make_async_remote_copy(
-        w_hbm.at[ROWS - 1], w_in.at[1], i_send.at[1], i_recv.at[1], sibling, MESH_ID)
-    i_w.start()
-    relay = pltpu.make_async_remote_copy(
-        w_in.at[1], w_in.at[0], i_send.at[3], i_recv.at[3], along(2), MESH_ID)
-    say(0)
+        w_hbm.at[ROWS - 1], w_in, i_send.at[1], i_recv.at[1], next_il, MESH_ID)
+    i_g = pltpu.make_async_remote_copy(g_out, g_in, i_send.at[2], i_recv.at[2], next_il, MESH_ID)
+    x_u = pltpu.make_async_remote_copy(
+        xl_u_out, xl_u_in, x_send.at[0], x_recv.at[0], prev_xl, MESH_ID)
+    x_f = pltpu.make_async_remote_copy(
+        xl_f_out, xl_f_in, x_send.at[1], x_recv.at[1], next_xl, MESH_ID)
+    pl.when(has_next_il)(i_w.start)
+    pl.when(has_prev_il)(i_u.start)
 
     lane = lax.broadcasted_iota(jnp.int32, (8, NT), 1)
     sub = lax.broadcasted_iota(jnp.int32, (8, NT), 0)
@@ -84,7 +95,7 @@
         return 0.5 * (ahead - behind)
 
     loads[0].wait()
-    loads[1].wait()
+    loads[2].wait()
 
     def lean(jb, _):
         rows = pl.ds(pl.multiple_of(jb * 8, 8), 8)
@@ -92,37 +103,34 @@
         g_out[rows] = here + sil[ROWS - 1, rows] * diff_t(here)
         return 0
     lax.fori_loop(0, STRIPS, lean, 0, unroll=True)
-    i_g = pltpu.make_async_remote_copy(g_out, g_in, i_send.at[2], i_recv.at[2], next_il, MESH_ID)
-    i_g.start()
-
-    @pl.when(core == 0)
-    def _():
-        i_w.wait_recv()
-        relay.start()
-
+    pl.when(has_next_il)(i_g.start)
+    loads[4].start()
+    loads[5].start()
 
     for i in range(ROWS):
         xl_u_out[i:i + 1] = u[i, 0:1]
-    x_u = pltpu.make_async_remote_copy(
-        xl_u_out, xl_u_in, x_send.at[0], x_recv.at[0], prev_xl, MESH_ID)
-    x_u.start()
-    loads[2].wait()
+    pl.when(has_prev_xl)(x_u.start)
+    loads[1].wait()
     loads[3].wait()
     for i in range(ROWS):
         tail = slice(COLS - 8, COLS)
         g = u[i, tail] + sxl[i, tail] * diff_t(u[i, tail])
         xl_f_out[i:i + 1] = g[7:8]
         xl_f_out[ROWS + i:ROWS + i + 1] = w[i, tail][7:8]
-    x_f = pltpu.make_async_remote_copy(
-        xl_f_out, xl_f_in, x_send.at[1], x_recv.at[1], next_xl, MESH_ID)
-    x_f.start()
+    pl.when(has_next_xl)(x_f.start)
     hear(0)
     say(1)
-
-    keep_il = jnp.where(il == NIL - 1, 0.0, 1.0).astype(F32)
-    keep_xl = jnp.where(xl == NXL - 1, 0.0, 1.0).astype(F32)
-    had_il = jnp.where(il == 0, 0.0, 1.0).astype(F32)
-    had_xl = jnp.where(xl == 0, 0.0, 1.0).astype(F32)
+    hear(3)
+    say(4)
+
+    for has, buffers in ((has_next_il, (u_in,)), (has_prev_il, (w_in, g_in)),
+                         (has_next_xl, (xl_u_in,)), (has_prev_xl, (xl_f_in,))):
+        @pl.when(jnp.logical_not(has))
+        def _(buffers=buffers):
+            for buffer in buffers:
+                buffer[...] = jnp.zeros_like(buffer)
+
+    keep_il, keep_xl = has_next_il.astype(F32), has_next_xl.astype(F32)
 
     def put_strip(i, jb, next_row, last=False):
         start = pl.multiple_of(jb * 8, 8)
@@ -153,14 +161,16 @@
 
     hear(1)
     say(2)
-
-    x_u.wait_recv()
+    hear(4)
+    say(5)
+
+    pl.when(has_next_xl)(x_u.wait_recv)
     for i in range(ROWS):
         put_strip(i, STRIPS - 1, xl_u_in[i:i + 1], True)
-    x_f.wait_recv()
+    pl.when(has_prev_xl)(x_f.wait_recv)
     for i in range(ROWS):
         wt = xl_f_in[ROWS + i:ROWS + i + 1]
-        fx[i, 7:8] = had_xl * (wt * wt * (u[i, 0:1] - xl_f_in[i:i + 1]))
+        fx[i, 7:8] = wt * wt * (u[i, 0:1] - xl_f_in[i:i + 1])
     loads[4].wait()
 
     def image_strip(i, jb, sums):
@@ -169,8 +179,8 @@
         fx_behind = jnp.where(first_r, fx[i, pl.ds(jb * 8 + 7, 1)], pltpu.roll(fx_here, 1, 0))
         here = u[i, rows]
         if i == 0:
-            wt = w_in[core, rows]
-            before = had_il * (wt * wt * (here - g_in[rows]))
+            wt = w_in[rows]
+            before = wt * wt * (here - g_in[rows])
         else:
             before = fil[i - 1, rows]
         q = (before - fil[i, rows]) + (fx_behind - fx_here) + diff_t(h[i, rows]) + damping * here
@@ -186,7 +196,7 @@
     for i in range(1, ROWS - 1):
         sums = image_inline(i, sums)
 
-    i_u.wait_recv()
+    pl.when(has_next_il)(i_u.wait_recv)
 
     def last_inline(jb, _):
         rows = pl.ds(pl.multiple_of(jb * 8, 8), 8)
@@ -198,17 +208,13 @@
     lax.fori_loop(0, STRIPS, last_inline, 0, unroll=True)
     sums = image_inline(ROWS - 1, sums)
 
-    @pl.when(core == 0)
-    def _():
-        relay.wait_recv()
-
-    @pl.when(core == 1)
+    @pl.when(has_prev_il)
     def _():
         i_w.wait_recv()
-
-    i_g.wait_recv()
+        i_g.wait_recv()
+
     sums = image_inline(0, sums)
-    hear(2)
+    hear(5)
 
     lane1 = lax.broadcasted_iota(jnp.int32, (8, 128), 1)
     row = jnp.zeros((8, 128), F32)
@@ -221,11 +227,10 @@
 
     near = lambda by, size: min(by, size - by)
     plane = [(dx, dy, 0, 0) for dx in range(4) for dy in range(8) if dx + dy > 0]
-    plane.sort(key=lambda p: -near(p[0], 4) - near(p[1], 8))
-    line = [(0, 0, dz, dc) for dz in range(8) for dc in range(2) if dz + dc > 0]
-    line.sort(key=lambda p: -near(p[2], 8))
+    plane.sort(key=lambda p: near(p[0], 4) + near(p[1], 8))
+    line = [(0, 0, dz, dc) for dz in (1, 2, 3, 4, 7, 6, 5, 0) for dc in range(2) if dz + dc > 0]
     drains = []
-    for phase, (offsets, box) in enumerate(((plane, box_xy), (line, box_zc))):
+    for phase, (offsets, box) in enumerate(((line, box_zc), (plane, box_xy))):
         count = len(offsets)
         msg[phase, 0:1] = row
         box[count:count + 1] = row
@@ -238,6 +243,8 @@
             box.at[pl.ds(0, count)], box.at[pl.ds(0, count)],
             r_send.at[phase], r_recv.at[phase], sibling, MESH_ID))
         drains[phase].wait_recv()
+        if phase == 0:
+            hear(2)
         row = jnp.sum(box[...], axis=0, keepdims=True)
 
     full = jnp.broadcast_to(row, (8, 128))
@@ -247,12 +254,11 @@
     beta = (rr - 2.0 * alpha * rq + alpha * alpha * qq) / rr
     coef[...] = jnp.where(lax.broadcasted_iota(jnp.int32, (8, 128), 0) == 0, alpha, beta)
 
-    for copy in (i_u, i_w, i_g, x_u, x_f):
-        copy.wait_send()
-
-    @pl.when(core == 0)
-    def _():
-        relay.wait_send()
+    for has, copies in ((has_prev_il, (i_u,)), (has_next_il, (i_w, i_g)), (has_prev_xl, (x_u,)), (has_next_xl, (x_f,))):
+        @pl.when(has)
+        def _(copies=copies):
+            for copy in copies:
+                copy.wait_send()
 
     for drain in drains:
         drain.wait_send()
@@ -274,11 +280,11 @@
         scratch_shapes=[
             pltpu.VMEM(shape, F32)
             for shape in (
-                block, block, block, block, (ROWS, COLS + 8, NT), block, plane, (2,) + plane, plane, plane,
+                block, block, block, block, (ROWS, COLS + 8, NT), block, plane, plane, plane, plane,
                 line, line, (2 * ROWS, NT), (2 * ROWS, NT), (2, 8, 128), (32, 128), (16, 128))
         ] + [
-            dma((6,)), dma((4,)), dma((4,)), dma((2,)), dma((2,)), dma((2,)), dma((2,)),
-            pltpu.SemaphoreType.REGULAR((3,))],
+            dma((6,)), dma((3,)), dma((3,)), dma((2,)), dma((2,)), dma((2,)), dma((2,)),
+            pltpu.SemaphoreType.REGULAR((6,))],
         compiler_params=pltpu.CompilerParams(
             collective_id=0, has_side_effects=True, vmem_limit_bytes=24 * 2**20),
     )(*operands)

time: 32.5 us -> 31.7 us (0.975)
  Pallas kernels: 31.7 us -> 30.9 us
    pallas_call x1, Pallas kernels: 30.5 us -> 29.7 us  [apply(): pl.pallas_call(kernel, out_shape=(jax.ShapeDtypeStruct(block, F32),) * 4...]
where the time goes in v4:
time: 31.7 us; the launch traced here: 31.6 us
  Pallas kernels  30.9 us (97%)
  between operations  0.64 us (2%)
    pallas_call x1, Pallas kernels, apply(): pl.pallas_call(kernel, out_shape=(jax.ShapeDtypeStruct(block, F32),) * 4...  29.7 us
    pallas_call x1, Pallas kernels, update(): pl.pallas_call(update_kernel, out_shape=(jax.ShapeDtypeStruct(block, F32)...  1.27 us

profile of v4, /device:TPU:1, one launch (start us, length us, event | category | flops | bytes accessed | tf_op | source)
XLA Modules:
  0.0 31.6 jit_solution(17836037772647629107)
XLA Ops:
  0.6 29.7 %shard_map.85 = (f32[4,64,512]{2,1,0:T(8,128)S(1)}, f32[4,64,512]{2,1,0:T(8,128)S(1)}, f32[4,64,512]{2,1,0:T(8,128)S(1)}, f32[4,64,512]{2,1,0:T(8,128)S(1)}, f32[8,128]{1,0:T(8,128)S(1)}) custom-call(f32[4,64,512]{2,1,0:T(8,128)} %sol_hbm.1, f32[4,64,512]{2,1,0:T(8,128)} %res_hbm.1, f32[4,64,512]{2,1,0:T(8,128)} %u_hbm.1, f32[4,64,512]{2,1,0:T(8,128)} %sil_hbm.1, ...), custom_call_target="tpu_custom_call" | custom-call | tf_op jit(solution)/shard_map/pallas_call | solution.py:275
  30.3 1.3 %shard_map.86 = (f32[4,64,512]{2,1,0:T(8,128)}, f32[4,64,512]{2,1,0:T(8,128)}, f32[4,64,512]{2,1,0:T(8,128)}) custom-call(f32[4,64,512]{2,1,0:T(8,128)S(1)} %get-tuple-element.8.sol, f32[4,64,512]{2,1,0:T(8,128)S(1)} %get-tuple-element.9.res, f32[4,64,512]{2,1,0:T(8,128)S(1)} %get-tuple-element.10.u, f32[4,64,512]{2,1,0:T(8,128)S(1)} %get-tuple-element.11.image, ...), custom_call_target="tpu_custom_call" | custom-call | tf_op jit(solution)/shard_map/pallas_call | solution.py:319

commit v5 on v4

--- a/solution.py
+++ b/solution.py
@@ -17,9 +17,9 @@
 def kernel(
     sol_hbm, res_hbm, u_hbm, sil_hbm, sxl_hbm, w_hbm,
     sol, res, u, image, coef,
-    sil, sxl, w, fil, fx, h, u_in, w_in, g_out, g_in, xl_u_out, xl_u_in, xl_f_out, xl_f_in,
+    sil, sxl, w, fil, fx, h, u_in, w_in, g_out, g_in, st_w, st_g, xl_u_out, xl_u_in, xl_f_out, xl_f_in,
     msg, box_xy, box_zc,
-    load_sem, i_send, i_recv, x_send, x_recv, r_send, r_recv, go,
+    load_sem, i_send, i_recv, s_send, s_recv, x_send, x_recv, r_send, r_recv, go,
 ):
     il, xl = lax.axis_index("il"), lax.axis_index("xl")
     z_hi, y, core = il // 16, (il // 2) % 8, il % 2
@@ -34,12 +34,21 @@
     next_xl, prev_xl = (il, (xl + 1) % NXL), (il, (xl + NXL - 1) % NXL)
     has_next_il, has_prev_il = il < NIL - 1, il > 0
     has_next_xl, has_prev_xl = xl < NXL - 1, xl > 0
+    last_y, first_y = jnp.logical_and(y == 7, core == 1), jnp.logical_and(y == 0, core == 0)
+    wrap_next = jnp.logical_and(last_y, has_next_il)
+    wrap_prev = jnp.logical_and(first_y, has_prev_il)
+    is_stage = jnp.logical_and(last_y, jnp.logical_and(z > 0, z < 7))
+    near_next = jnp.logical_and(has_next_il, jnp.logical_not(wrap_next))
+    near_prev = jnp.logical_and(has_prev_il, jnp.logical_not(wrap_prev))
+    stage, my_stage, staged = at(dz=1), at(dy=7, dz=7, dc=1), at(dy=1, dz=1, dc=1)
     sibling = at(dc=1)
 
     barrier = pltpu.get_barrier_semaphore()
     flat, deep = [at(dx=1), at(dx=3), at(dy=1), at(dy=7)], [at(dz=1), at(dz=7)]
     mesh_peers = (
-        (has_next_il, next_il), (has_prev_il, prev_il), (has_next_xl, next_xl), (has_prev_xl, prev_xl))
+        (has_next_il, next_il), (near_prev, prev_il), (has_next_xl, next_xl), (has_prev_xl, prev_xl),
+        (wrap_prev, my_stage))
+    heard = (has_prev_il, near_next, has_prev_xl, has_next_xl, is_stage)
     steps = (
         flat, [at(dy=2), at(dy=6)], [at(dx=1), at(dx=2), at(dx=3)],
         deep, [at(dz=2), at(dz=6)], [sibling],
@@ -66,7 +75,7 @@
     for load in loads[:4]:
         load.start()
     count = len(flat + deep)
-    for has, _ in mesh_peers:
+    for has in heard:
         count = count + has.astype(jnp.int32)
     pl.semaphore_wait(barrier, count)
     say(0)
@@ -74,14 +83,36 @@
 
     i_u = pltpu.make_async_remote_copy(
         u_hbm.at[0], u_in, i_send.at[0], i_recv.at[0], prev_il, MESH_ID)
-    i_w = pltpu.make_async_remote_copy(
-        w_hbm.at[ROWS - 1], w_in, i_send.at[1], i_recv.at[1], next_il, MESH_ID)
-    i_g = pltpu.make_async_remote_copy(g_out, g_in, i_send.at[2], i_recv.at[2], next_il, MESH_ID)
+    half = COLS // 2
+
+    def piece(k, weights, leaning):
+        return (weights if k < 2 else leaning).at[pl.ds(k % 2 * half, half)]
+
+    def copy_of(k, source, target, send_sem, recv_sem, device):
+        return pltpu.make_async_remote_copy(
+            piece(k, *source), piece(k, *target), send_sem, recv_sem, device, MESH_ID)
+
+    mine, theirs, passing = (w_hbm.at[ROWS - 1], g_out), (w_in, g_in), (st_w, st_g)
+    near = [copy_of(k, mine, theirs, i_send.at[1 + k], i_recv.at[1 + k], next_il) for k in range(4)]
+    far = [copy_of(k, mine, passing, i_send.at[1 + k], s_recv.at[k], stage) for k in range(4)]
+    relay = [copy_of(k, passing, theirs, s_send.at[k], i_recv.at[1 + k], staged) for k in range(4)]
+
+    def send(k):
+        pl.when(near_next)(near[k].start)
+        pl.when(wrap_next)(far[k].start)
+
+    def pass_on(k):
+        @pl.when(is_stage)
+        def _():
+            far[k].wait_recv()
+            relay[k].start()
+
     x_u = pltpu.make_async_remote_copy(
         xl_u_out, xl_u_in, x_send.at[0], x_recv.at[0], prev_xl, MESH_ID)
     x_f = pltpu.make_async_remote_copy(
         xl_f_out, xl_f_in, x_send.at[1], x_recv.at[1], next_xl, MESH_ID)
-    pl.when(has_next_il)(i_w.start)
+    pl.when(near_next)(near[0].start)
+    send(1)
     pl.when(has_prev_il)(i_u.start)
 
     lane = lax.broadcasted_iota(jnp.int32, (8, NT), 1)
@@ -102,8 +133,10 @@
         here = u[ROWS - 1, rows]
         g_out[rows] = here + sil[ROWS - 1, rows] * diff_t(here)
         return 0
-    lax.fori_loop(0, STRIPS, lean, 0, unroll=True)
-    pl.when(has_next_il)(i_g.start)
+    lax.fori_loop(0, STRIPS // 2, lean, 0, unroll=True)
+    send(2)
+    lax.fori_loop(STRIPS // 2, STRIPS, lean, 0, unroll=True)
+    send(3)
     loads[4].start()
     loads[5].start()
 
@@ -121,6 +154,7 @@
     hear(0)
     say(1)
     hear(3)
+    pl.when(wrap_next)(near[0].start)
     say(4)
 
     for has, buffers in ((has_next_il, (u_in,)), (has_prev_il, (w_in, g_in)),
@@ -159,10 +193,13 @@
             return 0
         lax.fori_loop(0, STRIPS - 1, strip, 0, unroll=True)
 
+    pass_on(1)
     hear(1)
     say(2)
     hear(4)
     say(5)
+    pass_on(2)
+    pass_on(3)
 
     pl.when(has_next_xl)(x_u.wait_recv)
     for i in range(ROWS):
@@ -210,8 +247,8 @@
 
     @pl.when(has_prev_il)
     def _():
-        i_w.wait_recv()
-        i_g.wait_recv()
+        for k in range(4):
+            near[k].wait_recv()
 
     sums = image_inline(0, sums)
     hear(5)
@@ -225,10 +262,19 @@
         row = jnp.where(lane1 // 32 == k, v, row)
     row = jnp.sum(row, axis=0, keepdims=True)
 
-    near = lambda by, size: min(by, size - by)
+    hops = lambda by, size: min(by, size - by)
     plane = [(dx, dy, 0, 0) for dx in range(4) for dy in range(8) if dx + dy > 0]
-    plane.sort(key=lambda p: near(p[0], 4) + near(p[1], 8))
+    plane.sort(key=lambda p: -hops(p[0], 4) - hops(p[1], 8))
     line = [(0, 0, dz, dc) for dz in (1, 2, 3, 4, 7, 6, 5, 0) for dc in range(2) if dz + dc > 0]
+    def finish():
+        for has, copies in ((has_prev_il, [i_u]), (has_next_il, near), (has_prev_xl, [x_u]), (has_next_xl, [x_f]),
+                            (is_stage, relay[1:])):
+            @pl.when(has)
+            def _(copies=copies):
+                for copy in copies:
+                    copy.wait_send()
+        loads[5].wait()
+
     drains = []
     for phase, (offsets, box) in enumerate(((line, box_zc), (plane, box_xy))):
         count = len(offsets)
@@ -242,6 +288,9 @@
         drains.append(pltpu.make_async_remote_copy(
             box.at[pl.ds(0, count)], box.at[pl.ds(0, count)],
             r_send.at[phase], r_recv.at[phase], sibling, MESH_ID))
+        drains[phase].wait_send()
+        if phase == 1:
+            finish()
         drains[phase].wait_recv()
         if phase == 0:
             hear(2)
@@ -253,16 +302,6 @@
     alpha = rr / dq
     beta = (rr - 2.0 * alpha * rq + alpha * alpha * qq) / rr
     coef[...] = jnp.where(lax.broadcasted_iota(jnp.int32, (8, 128), 0) == 0, alpha, beta)
-
-    for has, copies in ((has_prev_il, (i_u,)), (has_next_il, (i_w, i_g)), (has_prev_xl, (x_u,)), (has_next_xl, (x_f,))):
-        @pl.when(has)
-        def _(copies=copies):
-            for copy in copies:
-                copy.wait_send()
-
-    for drain in drains:
-        drain.wait_send()
-    loads[5].wait()
 
 
 def apply(solution, residual, direction, slope_il, slope_xl, weights):
@@ -280,10 +319,10 @@
         scratch_shapes=[
             pltpu.VMEM(shape, F32)
             for shape in (
-                block, block, block, block, (ROWS, COLS + 8, NT), block, plane, plane, plane, plane,
+                block, block, block, block, (ROWS, COLS + 8, NT), block, plane, plane, plane, plane, plane, plane,
                 line, line, (2 * ROWS, NT), (2 * ROWS, NT), (2, 8, 128), (32, 128), (16, 128))
         ] + [
-            dma((6,)), dma((3,)), dma((3,)), dma((2,)), dma((2,)), dma((2,)), dma((2,)),
+            dma((6,)), dma((5,)), dma((5,)), dma((4,)), dma((4,)), dma((2,)), dma((2,)), dma((2,)), dma((2,)),
             pltpu.SemaphoreType.REGULAR((6,))],
         compiler_params=pltpu.CompilerParams(
             collective_id=0, has_side_effects=True, vmem_limit_bytes=24 * 2**20),

time: 31.7 us -> 31.2 us (0.984)
  Pallas kernels: 30.9 us -> 30.4 us
    pallas_call x1, Pallas kernels: 29.7 us -> 29.2 us  [apply(): pl.pallas_call(kernel, out_shape=(jax.ShapeDtypeStruct(block, F32),) * 4...]
where the time goes in v5:
time: 31.2 us; the launch traced here: 31.1 us
  Pallas kernels  30.4 us (97%)
  between operations  0.64 us (2%)
    pallas_call x1, Pallas kernels, apply(): pl.pallas_call(kernel, out_shape=(jax.ShapeDtypeStruct(block, F32),) * 4...  29.2 us
    pallas_call x1, Pallas kernels, update(): pl.pallas_call(update_kernel, out_shape=(jax.ShapeDtypeStruct(block, F32)...  1.27 us

profile of v5, /device:TPU:1, one launch (start us, length us, event | category | flops | bytes accessed | tf_op | source)
XLA Modules:
  0.0 31.1 jit_solution(5854952654567680324)
XLA Ops:
  0.6 29.2 %shard_map.85 = (f32[4,64,512]{2,1,0:T(8,128)S(1)}, f32[4,64,512]{2,1,0:T(8,128)S(1)}, f32[4,64,512]{2,1,0:T(8,128)S(1)}, f32[4,64,512]{2,1,0:T(8,128)S(1)}, f32[8,128]{1,0:T(8,128)S(1)}) custom-call(f32[4,64,512]{2,1,0:T(8,128)} %sol_hbm.1, f32[4,64,512]{2,1,0:T(8,128)} %res_hbm.1, f32[4,64,512]{2,1,0:T(8,128)} %u_hbm.1, f32[4,64,512]{2,1,0:T(8,128)} %sil_hbm.1, ...), custom_call_target="tpu_custom_call" | custom-call | tf_op jit(solution)/shard_map/pallas_call | solution.py:314
  29.8 1.3 %shard_map.86 = (f32[4,64,512]{2,1,0:T(8,128)}, f32[4,64,512]{2,1,0:T(8,128)}, f32[4,64,512]{2,1,0:T(8,128)}) custom-call(f32[4,64,512]{2,1,0:T(8,128)S(1)} %get-tuple-element.8.sol, f32[4,64,512]{2,1,0:T(8,128)S(1)} %get-tuple-element.9.res, f32[4,64,512]{2,1,0:T(8,128)S(1)} %get-tuple-element.10.u, f32[4,64,512]{2,1,0:T(8,128)S(1)} %get-tuple-element.11.image, ...), custom_call_target="tpu_custom_call" | custom-call | tf_op jit(solution)/shard_map/pallas_call | solution.py:358

commit v6 on v5

--- a/solution.py
+++ b/solution.py
@@ -21,6 +21,13 @@
     msg, box_xy, box_zc,
     load_sem, i_send, i_recv, s_send, s_recv, x_send, x_recv, r_send, r_recv, go,
 ):
+    loads = [
+        pltpu.make_async_copy(source, target, load_sem.at[k])
+        for k, (source, target) in enumerate((
+            (u_hbm, u), (w_hbm, w), (sil_hbm, sil), (sxl_hbm, sxl), (res_hbm, res), (sol_hbm, sol)))
+    ]
+    for load in loads[:4]:
+        load.start()
     il, xl = lax.axis_index("il"), lax.axis_index("xl")
     z_hi, y, core = il // 16, (il // 2) % 8, il % 2
     z_lo, x = xl // 4, xl % 4
@@ -67,13 +74,6 @@
     def hear(step):
         pl.semaphore_wait(go.at[step], len(steps[step]))
 
-    loads = [
-        pltpu.make_async_copy(source, target, load_sem.at[k])
-        for k, (source, target) in enumerate((
-            (u_hbm, u), (w_hbm, w), (sil_hbm, sil), (sxl_hbm, sxl), (res_hbm, res), (sol_hbm, sol)))
-    ]
-    for load in loads[:4]:
-        load.start()
     count = len(flat + deep)
     for has in heard:
         count = count + has.astype(jnp.int32)
@@ -82,7 +82,7 @@
     say(3)
 
     i_u = pltpu.make_async_remote_copy(
-        u_hbm.at[0], u_in, i_send.at[0], i_recv.at[0], prev_il, MESH_ID)
+        u.at[0], u_in, i_send.at[0], i_recv.at[0], prev_il, MESH_ID)
     half = COLS // 2
 
     def piece(k, weights, leaning):
@@ -92,7 +92,7 @@
         return pltpu.make_async_remote_copy(
             piece(k, *source), piece(k, *target), send_sem, recv_sem, device, MESH_ID)
 
-    mine, theirs, passing = (w_hbm.at[ROWS - 1], g_out), (w_in, g_in), (st_w, st_g)
+    mine, theirs, passing = (w.at[ROWS - 1], g_out), (w_in, g_in), (st_w, st_g)
     near = [copy_of(k, mine, theirs, i_send.at[1 + k], i_recv.at[1 + k], next_il) for k in range(4)]
     far = [copy_of(k, mine, passing, i_send.at[1 + k], s_recv.at[k], stage) for k in range(4)]
     relay = [copy_of(k, passing, theirs, s_send.at[k], i_recv.at[1 + k], staged) for k in range(4)]
@@ -111,9 +111,11 @@
         xl_u_out, xl_u_in, x_send.at[0], x_recv.at[0], prev_xl, MESH_ID)
     x_f = pltpu.make_async_remote_copy(
         xl_f_out, xl_f_in, x_send.at[1], x_recv.at[1], next_xl, MESH_ID)
+    loads[0].wait()
+    pl.when(has_prev_il)(i_u.start)
+    loads[1].wait()
     pl.when(near_next)(near[0].start)
     send(1)
-    pl.when(has_prev_il)(i_u.start)
 
     lane = lax.broadcasted_iota(jnp.int32, (8, NT), 1)
     sub = lax.broadcasted_iota(jnp.int32, (8, NT), 0)
@@ -125,7 +127,6 @@
         behind = jnp.where(first_t, 0.0, pltpu.roll(v, 1, 1))
         return 0.5 * (ahead - behind)
 
-    loads[0].wait()
     loads[2].wait()
 
     def lean(jb, _):
@@ -143,7 +144,6 @@
     for i in range(ROWS):
         xl_u_out[i:i + 1] = u[i, 0:1]
     pl.when(has_prev_xl)(x_u.start)
-    loads[1].wait()
     loads[3].wait()
     for i in range(ROWS):
         tail = slice(COLS - 8, COLS)

time: 31.2 us -> 31 us (level)
  no operation moved by 1% of the time
where the time goes in v6:
time: 31 us; the launch traced here: 30.9 us
  Pallas kernels  30.2 us (97%)
  between operations  0.64 us (2%)
    pallas_call x1, Pallas kernels, apply(): pl.pallas_call(kernel, out_shape=(jax.ShapeDtypeStruct(block, F32),) * 4...  29 us
    pallas_call x1, Pallas kernels, update(): pl.pallas_call(update_kernel, out_shape=(jax.ShapeDtypeStruct(block, F32)...  1.27 us

profile of v6, /device:TPU:1, one launch (start us, length us, event | category | flops | bytes accessed | tf_op | source)
XLA Modules:
  0.0 30.9 jit_solution(6920329411410387090)
XLA Ops:
  0.6 29.0 %shard_map.85 = (f32[4,64,512]{2,1,0:T(8,128)S(1)}, f32[4,64,512]{2,1,0:T(8,128)S(1)}, f32[4,64,512]{2,1,0:T(8,128)S(1)}, f32[4,64,512]{2,1,0:T(8,128)S(1)}, f32[8,128]{1,0:T(8,128)S(1)}) custom-call(f32[4,64,512]{2,1,0:T(8,128)} %sol_hbm.1, f32[4,64,512]{2,1,0:T(8,128)} %res_hbm.1, f32[4,64,512]{2,1,0:T(8,128)} %u_hbm.1, f32[4,64,512]{2,1,0:T(8,128)} %sil_hbm.1, ...), custom_call_target="tpu_custom_call" | custom-call | tf_op jit(solution)/shard_map/pallas_call | solution.py:314
  29.6 1.3 %shard_map.86 = (f32[4,64,512]{2,1,0:T(8,128)}, f32[4,64,512]{2,1,0:T(8,128)}, f32[4,64,512]{2,1,0:T(8,128)}) custom-call(f32[4,64,512]{2,1,0:T(8,128)S(1)} %get-tuple-element.8.sol, f32[4,64,512]{2,1,0:T(8,128)S(1)} %get-tuple-element.9.res, f32[4,64,512]{2,1,0:T(8,128)S(1)} %get-tuple-element.10.u, f32[4,64,512]{2,1,0:T(8,128)S(1)} %get-tuple-element.11.image, ...), custom_call_target="tpu_custom_call" | custom-call | tf_op jit(solution)/shard_map/pallas_call | solution.py:358

commit v7 on v6

--- a/solution.py
+++ b/solution.py
@@ -226,8 +226,8 @@
         rr, dq, rq, qq = sums
         return rr + r * r, dq + here * q, rq + r * q, qq + q * q
 
-    def image_inline(i, sums):
-        return lax.fori_loop(0, STRIPS, lambda jb, s: image_strip(i, jb, s), sums, unroll=True)
+    def image_inline(i, sums, start=0, stop=STRIPS):
+        return lax.fori_loop(start, stop, lambda jb, s: image_strip(i, jb, s), sums, unroll=True)
 
     sums = tuple(jnp.zeros((8, NT), F32) for _ in range(4))
     for i in range(1, ROWS - 1):
@@ -245,12 +245,13 @@
     lax.fori_loop(0, STRIPS, last_inline, 0, unroll=True)
     sums = image_inline(ROWS - 1, sums)
 
-    @pl.when(has_prev_il)
-    def _():
-        for k in range(4):
-            near[k].wait_recv()
-
-    sums = image_inline(0, sums)
+    for part in range(2):
+        @pl.when(has_prev_il)
+        def _(part=part):
+            near[part].wait_recv()
+            near[2 + part].wait_recv()
+
+        sums = image_inline(0, sums, part * STRIPS // 2, (part + 1) * STRIPS // 2)
     hear(5)
 
     lane1 = lax.broadcasted_iota(jnp.int32, (8, 128), 1)

time: 31 us -> 31 us (level)
  no operation moved by 1% of the time
where the time goes in v7:
time: 31 us; the launch traced here: 30.8 us
  Pallas kernels  30.2 us (97%)
  between operations  0.64 us (2%)
    pallas_call x1, Pallas kernels, apply(): pl.pallas_call(kernel, out_shape=(jax.ShapeDtypeStruct(block, F32),) * 4...  28.9 us
    pallas_call x1, Pallas kernels, update(): pl.pallas_call(update_kernel, out_shape=(jax.ShapeDtypeStruct(block, F32)...  1.27 us

profile of v7, /device:TPU:1, one launch (start us, length us, event | category | flops | bytes accessed | tf_op | source)
XLA Modules:
  0.0 30.8 jit_solution(16495121191019979632)
XLA Ops:
  0.6 28.9 %shard_map.85 = (f32[4,64,512]{2,1,0:T(8,128)S(1)}, f32[4,64,512]{2,1,0:T(8,128)S(1)}, f32[4,64,512]{2,1,0:T(8,128)S(1)}, f32[4,64,512]{2,1,0:T(8,128)S(1)}, f32[8,128]{1,0:T(8,128)S(1)}) custom-call(f32[4,64,512]{2,1,0:T(8,128)} %sol_hbm.1, f32[4,64,512]{2,1,0:T(8,128)} %res_hbm.1, f32[4,64,512]{2,1,0:T(8,128)} %u_hbm.1, f32[4,64,512]{2,1,0:T(8,128)} %sil_hbm.1, ...), custom_call_target="tpu_custom_call" | custom-call | tf_op jit(solution)/shard_map/pallas_call | solution.py:315
  29.6 1.3 %shard_map.86 = (f32[4,64,512]{2,1,0:T(8,128)}, f32[4,64,512]{2,1,0:T(8,128)}, f32[4,64,512]{2,1,0:T(8,128)}) custom-call(f32[4,64,512]{2,1,0:T(8,128)S(1)} %get-tuple-element.8.sol, f32[4,64,512]{2,1,0:T(8,128)S(1)} %get-tuple-element.9.res, f32[4,64,512]{2,1,0:T(8,128)S(1)} %get-tuple-element.10.u, f32[4,64,512]{2,1,0:T(8,128)S(1)} %get-tuple-element.11.image, ...), custom_call_target="tpu_custom_call" | custom-call | tf_op jit(solution)/shard_map/pallas_call | solution.py:359
